TPU v7x, 512 devices: a whole 4x4x16 slice. The times are simulated.
512 devices in a mesh: inline: 8 (over y, x_hi), window: 16 (over z), replica: 4 (over x_lo, core).
Axes of the slice: x: 4 (x_hi: 2, x_lo: 2; x = x_hi * 2 + x_lo), y: 4, z: 16, core: 2. Of those that a mesh axis runs over, the one named last changes fastest.
Arguments:
- tokens: bfloat16 [512, 128, 8, 512], P(('replica', 'inline', 'window')), parts along dimension 0, may hold values from -6 to 6
- probe_match_payload_matrix: bfloat16 [512, 1536], replicated, may hold values from -1.5 to 1.5
- w_out: bfloat16 [512, 512], replicated, may hold values from -0.25 to 0.25
Outputs:
- update: bfloat16 [512, 128, 8, 512], P(('replica', 'inline', 'window')), parts along dimension 0
There are 4 independent parts, one for each index of `replica`. A program takes and returns all parts, laid end to end along the dimension named above; an argument that names none is the same for every part. Nothing has to cross between parts.
All inputs are finite; a program needn't handle non-finite values.
Results may differ from a plain program's by a relative error of at most 0.012.
The roundings to bfloat16 on the way count: a program that leaves them out, or rounds other values in their place, can miss the bound.
Values may be sent and summed in bfloat16 or wider, within the bound.
No kernel may reach another device: no remote copies, remote signals or barrier semaphores. Data moves between devices by JAX's collectives and lax.ppermute only.
A program may use at most 64 MiB of HBM per device.

v0:
```python
import jax
import jax.numpy as jnp
from jax import lax
from jax.sharding import PartitionSpec as P

EMBED_SPAN = 512
FOCUS_GROUPS = 16
WIN = 8


EPSILON = 1e-05


def standardize_features(payload_vectors):
    center = payload_vectors - jnp.mean(payload_vectors, axis=-1, keepdims=True)
    spread = jnp.mean(center * center, axis=-1, keepdims=True)
    return center * lax.rsqrt(spread + EPSILON)


def to_windows(block):
    first, second, third, width = block.shape
    shaped = block.reshape(first // WIN, WIN, second // WIN, WIN, third // WIN, WIN, width)
    return shaped.transpose(0, 2, 4, 1, 3, 5, 6).reshape(-1, WIN * WIN * WIN, width)


def from_windows(cube_rows, first, second, third):
    width = cube_rows.shape[-1]
    shaped = cube_rows.reshape(first // WIN, second // WIN, third // WIN, WIN, WIN, WIN, width)
    return shaped.transpose(0, 3, 1, 4, 2, 5, 6).reshape(first, second, third, width)


def ingest_summary(running_state, condensed_question_series, lookup_arrays, payload_vectors):
    top_old, total_old, summed_old = running_state
    reduced_dimension = EMBED_SPAN // FOCUS_GROUPS
    softmax_sharpness = reduced_dimension ** (-0.5)
    probe_split = condensed_question_series.reshape(
        condensed_question_series.shape[0], FOCUS_GROUPS, reduced_dimension
    )
    lookup_divided = lookup_arrays.reshape(lookup_arrays.shape[0], FOCUS_GROUPS, reduced_dimension)
    payload_split = payload_vectors.reshape(
        payload_vectors.shape[0], FOCUS_GROUPS, reduced_dimension
    )
    similarity_raw_scores = (
        jnp.einsum("xjr,ijr->jxi", probe_split, lookup_divided, preferred_element_type=jnp.float32)
        * softmax_sharpness
    )
    top_new = jnp.maximum(top_old, jnp.max(similarity_raw_scores, axis=-1))
    rescale = jnp.exp(top_old - top_new)
    weights = jnp.exp(similarity_raw_scores - top_new[..., None])
    total_new = jnp.sum(weights, axis=-1)
    added = jnp.einsum(
        "hqk,khd->qhd",
        weights.astype(jnp.bfloat16),
        payload_split,
        preferred_element_type=jnp.float32,
    )
    summed_new = summed_old * rescale.T[:, :, None] + added
    return (top_new, total_new, summed_new)


def tile_mixing(
    tile_items,
    probe_match_payload_matrix,
    digest_match_list,
    digest_payload_list,
    broad_contribution,
):
    count = tile_items.shape[0]
    reduced_dimension = EMBED_SPAN // FOCUS_GROUPS
    softmax_sharpness = reduced_dimension ** (-0.5)
    projected = jnp.dot(
        tile_items, probe_match_payload_matrix, preferred_element_type=jnp.float32
    ).astype(jnp.bfloat16)
    question_arrays = projected[:, :EMBED_SPAN].reshape(count, FOCUS_GROUPS, reduced_dimension)
    lookup_arrays = projected[:, EMBED_SPAN : 2 * EMBED_SPAN].reshape(
        count, FOCUS_GROUPS, reduced_dimension
    )
    payload_vectors = projected[:, 2 * EMBED_SPAN :].reshape(count, FOCUS_GROUPS, reduced_dimension)
    lookup_condensed = digest_match_list.reshape(FOCUS_GROUPS, reduced_dimension)
    payload_digest = digest_payload_list.reshape(FOCUS_GROUPS, reduced_dimension).astype(
        jnp.float32
    )
    per_group = FOCUS_GROUPS // 4
    results = []
    for head_group in range(4):
        bottom_bound = head_group * per_group
        ceiling_bound = bottom_bound + per_group
        similarity_raw_scores = (
            jnp.einsum(
                "xjr,ijr->jxi",
                question_arrays[:, bottom_bound:ceiling_bound],
                lookup_arrays[:, bottom_bound:ceiling_bound],
                preferred_element_type=jnp.float32,
            )
            * softmax_sharpness
        )
        courier_marks = (
            jnp.einsum(
                "yoc,oc->oy",
                question_arrays[:, bottom_bound:ceiling_bound],
                lookup_condensed[bottom_bound:ceiling_bound],
                preferred_element_type=jnp.float32,
            )
            * softmax_sharpness
        )
        top = jnp.maximum(jnp.max(similarity_raw_scores, axis=-1), courier_marks)
        weights = jnp.exp(similarity_raw_scores - top[..., None])
        car_weights = jnp.exp(courier_marks - top)
        total = jnp.sum(weights, axis=-1) + car_weights
        summed = jnp.einsum(
            "hqk,khd->qhd",
            weights.astype(jnp.bfloat16),
            payload_vectors[:, bottom_bound:ceiling_bound],
            preferred_element_type=jnp.float32,
        )
        car_rounded = car_weights.astype(jnp.bfloat16).astype(jnp.float32)
        summed = (
            summed
            + car_rounded.T[:, :, None] * payload_digest[bottom_bound:ceiling_bound][None, :, :]
        )
        results.append(summed / total.T[:, :, None])
    local = jnp.concatenate(results, axis=1).reshape(count, EMBED_SPAN)
    return (local + broad_contribution[None, :]).astype(jnp.bfloat16)


def body(tokens, probe_match_payload_matrix, w_out):
    reduced_dimension = EMBED_SPAN // FOCUS_GROUPS
    entry_rows, entry_cols, entry_depth, width = tokens.shape
    normed = standardize_features(tokens.astype(jnp.float32)).astype(jnp.bfloat16)
    grouped = lax.all_to_all(normed, "window", split_axis=1, concat_axis=0, tiled=True)
    block_rows, block_cols, block_depth, width = grouped.shape
    tile_entries = to_windows(grouped)
    own_count = tile_entries.shape[0]
    averaged_tiles = jnp.sum(tile_entries.astype(jnp.float32), axis=1) / (
        1.0 * tile_entries.shape[1]
    )
    digest_items = standardize_features(averaged_tiles).astype(jnp.bfloat16)
    digest_mapping = jnp.dot(
        digest_items, probe_match_payload_matrix, preferred_element_type=jnp.float32
    ).astype(jnp.bfloat16)
    condensed_question_series = digest_mapping[:, :EMBED_SPAN]
    digest_match_list = digest_mapping[:, EMBED_SPAN : 2 * EMBED_SPAN]
    digest_payload_list = digest_mapping[:, 2 * EMBED_SPAN :]
    initial_state = (
        jnp.full((FOCUS_GROUPS, own_count), -1e30, jnp.float32),
        jnp.zeros((FOCUS_GROUPS, own_count), jnp.float32),
        jnp.zeros((own_count, FOCUS_GROUPS, reduced_dimension), jnp.float32),
    )
    match_payload_pair = jnp.dot(
        lax.all_gather(digest_items, ("inline", "window"), axis=0, tiled=True),
        probe_match_payload_matrix[:, EMBED_SPAN:],
        preferred_element_type=jnp.float32,
    ).astype(jnp.bfloat16)
    folded = ingest_summary(
        initial_state,
        condensed_question_series,
        match_payload_pair[:, :EMBED_SPAN],
        match_payload_pair[:, EMBED_SPAN:],
    )
    broad_context = (folded[2] / folded[1].T[:, :, None]).reshape(own_count, EMBED_SPAN)

    def single_tile(window_item):
        return tile_mixing(
            window_item[0],
            probe_match_payload_matrix,
            window_item[1],
            window_item[2],
            window_item[3],
        )

    nested_step = lax.map(
        single_tile, (tile_entries, digest_match_list, digest_payload_list, broad_context)
    )
    projected = jnp.dot(
        nested_step.reshape(-1, width), w_out, preferred_element_type=jnp.float32
    ).astype(jnp.bfloat16)
    placed = from_windows(projected.reshape(nested_step.shape), block_rows, block_cols, block_depth)
    returned = lax.all_to_all(placed, "window", split_axis=0, concat_axis=1, tiled=True)
    return returned


def solution(mesh):
    return jax.shard_map(
        body,
        mesh=mesh,
        in_specs=(P(("replica", "inline", "window"), None, None, None), P(), P()),
        out_specs=P(("replica", "inline", "window"), None, None, None),
        check_vma=False,
    )
```

profile of v0, /device:TPU:32, one launch (start us, length us, event | category | flops | bytes accessed | tf_op | source)
XLA Modules:
  0.0 553.5 jit_solution(7632967294819496900)
XLA Ops:
  0.0 1.5 convert_reduce_fusion
  1.5 1.8 fusion.87
  3.3 2.6 fusion.88
  5.9 15.2 %all-to-all-start = ((bf16[1,128,8,512]{3,2,0,1:T(8,128)(2,1)}), bf16[1,128,8,512]{3,2,0,1:T(8,128)(2,1)}, u32[]{:S(2)}, u32[]{:S(2)}) async-start(bf16[1,128,8,512]{3,2,0,1:T(8,128)(2,1)} %fusion.88), calls=%async_computation | async-start | bytes 2097152 | tf_op jit(solution)/shard_map/all_to_all | solution.py:130
  21.1 49.3 %all-to-all-done = bf16[1,128,8,512]{3,2,0,1:T(8,128)(2,1)} async-done(((bf16[1,128,8,512]{3,2,0,1:T(8,128)(2,1)}), bf16[1,128,8,512]{3,2,0,1:T(8,128)(2,1)}, u32[]{:S(2)}, u32[]{:S(2)}) %all-to-all-start) | async-done | bytes 1048608 | tf_op jit(solution)/shard_map/all_to_all | solution.py:130
  70.4 1.9 convert_reduce_fusion.1
  72.8 1.8 convolution_convert_fusion.1
  74.7 351.9 %all-gather = bf16[128,2,512]{2,1,0:T(2,128)(2,1)S(1)} all-gather(bf16[1,2,512]{2,1,0:T(2,128)(2,1)S(1)} %fusion.129), channel_id=1, replica_groups=mesh['inline'=8,'window'=16,'replica'=4] {'inline','window'}, dimensions={0}, use_global_device_ids=true | all-gather | bytes 264192 | tf_op jit(solution)/shard_map/all_gather | solution.py:150
  426.7 1.7 convolution_convert_fusion.3
  428.5 0.2 fusion.100
  429.1 0.2 fusion.90
  429.4 80.8 %while.10 = (s32[]{:T(128)}, bf16[2,512,512]{2,1,0:T(8,128)(2,1)}, bf16[2,512,512]{2,1,0:T(8,128)(2,1)}, bf16[512,1536]{1,0:T(8,128)(2,1)}, bf16[2,512]{1,0:T(2,...) while((s32[]{:T(128)}, bf16[2,512,512]{2,1,0:T(8,128)(2,1)}, ...), condition=%wide.region_17.18_spmd, body=%wide.region_8.17_spmd.sunk | while | flops 1379189248 | bytes 74441896 | solution.py:171
  429.6 2.6 convolution_convert_fusion.5
  432.3 0.2 copy.136
  432.7 2.7 multiply_reduce_fusion.13
  435.7 2.9 fusion.209
  439.0 3.0 fusion.210
  441.9 2.7 multiply_reduce_fusion.12
  444.8 2.9 fusion.205
  447.8 3.0 fusion.206
  450.8 2.7 multiply_reduce_fusion.11
  453.7 2.9 fusion.201
  456.7 3.0 fusion.202
  459.7 2.7 multiply_reduce_fusion.10
  462.6 2.9 fusion.197
  465.6 3.0 fusion.198
  468.9 0.2 copy.138
  469.1 0.8 constant_dynamic-update-slice_fusion.2
  469.9 2.6 convolution_convert_fusion.5
  472.6 0.2 copy.136
  472.8 0.2 copy.137
  473.0 2.7 multiply_reduce_fusion.13
  476.1 2.9 fusion.209
  479.3 3.0 fusion.210
  482.3 2.7 multiply_reduce_fusion.12
  485.2 2.9 fusion.205
  488.2 3.0 fusion.206
  491.2 2.7 multiply_reduce_fusion.11
  494.1 2.9 fusion.201
  497.1 3.0 fusion.202
  500.1 2.7 multiply_reduce_fusion.10
  503.0 2.9 fusion.197
  506.0 3.0 fusion.198
  509.2 0.2 copy.138
  509.4 0.8 constant_dynamic-update-slice_fusion.2
  510.3 1.9 convolution_convert_fusion.2
  512.2 40.3 %all_to_all.21 = bf16[16,8,8,512]{3,2,1,0:T(8,128)(2,1)S(1)} all-to-all(bf16[16,8,8,512]{3,2,1,0:T(8,128)(2,1)S(1)} %bitcast.281), channel_id=1, replica_groups=mesh['inline'=8,'window'=16,'replica'=4] {'window'}, dimensions={0} | all-to-all | bytes 2097152 | tf_op jit(solution)/shard_map/all_to_all | solution.py:178
  552.5 1.0 copy.147
  (78 shorter events, 5.4 us)
Async XLA Ops:
  0.0 510.3 %copy-start = (bf16[512,512]{1,0:T(8,128)(2,1)S(1)}, bf16[512,512]{1,0:T(8,128)(2,1)}, u32[]{:S(2)}) copy-start(bf16[512,512]{1,0:T(8,128)(2,1)} %param.7) | copy-start | bytes 1572868
  5.9 64.6 %all-to-all-start = ((bf16[1,128,8,512]{3,2,0,1:T(8,128)(2,1)}), bf16[1,128,8,512]{3,2,0,1:T(8,128)(2,1)}, u32[]{:S(2)}, u32[]{:S(2)}) async-start(bf16[1,128,8,512]{3,2,0,1:T(8,128)(2,1)} %fusion.88), calls=%async_computation | async-start | bytes 2097152 | tf_op jit(solution)/shard_map/all_to_all | solution.py:130
where the time goes:
time: 555 us; the launch traced here: 554 us
  blocking collectives  392 us (71%)
  matrix products  57.3 us (10%)
  waiting for transfers between devices  49.3 us (9%)
  other arithmetic  32.2 us (6%)
  starting transfers between devices  15.2 us (3%)
  local copies, waits for them, and re-layouts  6.76 us (1%)
    all_gather x1, blocking collectives, body(): lax.all_gather(digest_items, ('inline', 'window'), axis=0, tiled=True)  352 us
    all_to_all x1, waiting for transfers between devices, body(): lax.all_to_all(normed, 'window', split_axis=1, concat_axis=0, tiled=True)  49.3 us
    all_to_all x1, blocking collectives, body(): lax.all_to_all(placed, 'window', split_axis=0, concat_axis=1, tiled=True)  40.3 us
    dot_general x8, matrix products, tile_mixing(): jnp.einsum('hqk,khd->qhd', weights.astype(jnp.bfloat16), payload_vectors[...  23.8 us
    reduce_sum x8, other arithmetic, tile_mixing(): total = jnp.sum(weights, axis=-1) + car_weights  23.2 us
    dot_general x8, matrix products, tile_mixing(): jnp.einsum('xjr,ijr->jxi', question_arrays[:, bottom_bound:ceiling_bound]...  21.5 us
    all_to_all x1, starting transfers between devices, body(): lax.all_to_all(normed, 'window', split_axis=1, concat_axis=0, tiled=True)  15.2 us
  transfers between devices with their start and end apart: 1, of which 1 were waited for; matrix products, arithmetic and copies ran while one was open for 0% of the time, Pallas kernels for 0%

commit v1 on v0

v1 whole, which is shorter than its diff:
```python
import jax
import jax.numpy as jnp
from jax import lax
from jax.experimental import pallas as pl
from jax.experimental.pallas import tpu as pltpu
from jax.sharding import PartitionSpec as P

EMBED_SPAN = 512
HEADS = 16
HEAD_DIM = EMBED_SPAN // HEADS
WIN = 8
EPSILON = 1e-05
LOG2E = 1.4426950408889634
SCALE = HEAD_DIM ** (-0.5)
F32 = jnp.float32
BF16 = jnp.bfloat16
VMEM_LIMIT = 48 * 1024 * 1024


def standardize(values):
    center = values - jnp.mean(values, axis=-1, keepdims=True)
    spread = jnp.mean(center * center, axis=-1, keepdims=True)
    return center * lax.rsqrt(spread + EPSILON)


def norm_kernel(x_ref, normed_ref, sums_ref):
    dests, tokens, width = x_ref.shape
    normed = standardize(x_ref[...].astype(F32)).astype(BF16)
    normed_ref[...] = normed
    cells = normed.astype(F32).reshape(dests * tokens // (WIN * WIN), WIN * WIN, width)
    sums_ref[...] = jnp.sum(cells, axis=1)


def carrier_kernel(sums_ref, out_ref):
    total = jnp.sum(sums_ref[...], axis=1)
    out_ref[...] = standardize(total * (1.0 / WIN**3)).astype(BF16).reshape(out_ref.shape)


def head_mask(rows):
    lane = lax.broadcasted_iota(jnp.int32, (rows, EMBED_SPAN), 1) // HEAD_DIM
    row = lax.broadcasted_iota(jnp.int32, (rows, EMBED_SPAN), 0) % HEADS
    return lane == row


def glob_kernel(all_ref, own_ref, w_ref, out_ref):
    own_count = own_ref.shape[0]
    match = jnp.dot(all_ref[...], w_ref[:, EMBED_SPAN:], preferred_element_type=F32).astype(BF16)
    keys, values = match[:, :EMBED_SPAN], match[:, EMBED_SPAN:]
    own = jnp.concatenate([own_ref[...].astype(F32), jnp.zeros((16 - own_count, EMBED_SPAN), F32)], axis=0).astype(BF16)
    proj = jnp.dot(own, w_ref[...], preferred_element_type=F32).astype(BF16).astype(F32)
    mask = head_mask(HEADS)
    for c in range(own_count):
        row = proj[c : c + 1]
        queries = jnp.where(mask, row[:, :EMBED_SPAN], 0.0).astype(BF16)
        s = lax.dot_general(queries, keys, (((1,), (1,)), ((), ())), preferred_element_type=F32) * SCALE
        weights = jnp.exp(s - jnp.max(s, axis=-1, keepdims=True))
        total = jnp.sum(weights, axis=-1, keepdims=True)
        summed = jnp.dot(weights.astype(BF16), values, preferred_element_type=F32) / total
        glob = jnp.sum(jnp.where(mask, summed, 0.0), axis=0, keepdims=True)
        out_ref[c] = jnp.concatenate(
            [glob, row[:, EMBED_SPAN : 2 * EMBED_SPAN], row[:, 2 * EMBED_SPAN :], jnp.zeros((5, EMBED_SPAN), F32)], axis=0
        )


def window_kernel(x_ref, aux_ref, wk_ref, wqt_ref, wvt_ref, wo_ref, out_ref, k_s, qh_s, ql_s, vt_s, sc_s, vc_s, gl_s, inner_s):
    count = WIN**3
    x = x_ref[...].reshape(count, EMBED_SPAN)
    nt = (((1,), (1,)), ((), ()))
    k_s[...] = jnp.dot(x, wk_ref[...], preferred_element_type=F32).astype(BF16)
    q = lax.dot_general(wqt_ref[...], x, nt, preferred_element_type=F32).astype(BF16).astype(F32) * (SCALE * LOG2E)
    high = q.astype(BF16)
    low = (q - high.astype(F32)).astype(BF16)
    qh_s[...] = high
    ql_s[...] = low
    vt_s[...] = lax.dot_general(wvt_ref[...], x, nt, preferred_element_type=F32).astype(BF16)
    aux = aux_ref[0]
    kc = jnp.where(head_mask(HEADS), aux[1:2], 0.0).astype(BF16)
    sc_s[...] = jnp.dot(kc, high, preferred_element_type=F32) + jnp.dot(kc, low, preferred_element_type=F32)
    gl_s[...] = jnp.broadcast_to(aux[0:1], (128, EMBED_SPAN)).T
    vc_s[...] = jnp.broadcast_to(aux[2:3], (128, EMBED_SPAN)).T
    ones = jnp.ones((16, count), BF16)

    def widen(column):
        return jnp.concatenate([column] * (count // 128), axis=1)

    def group(g, carry):
        lanes = pl.ds(pl.multiple_of(g * 128, 128), 128)
        kg = k_s[:, lanes]
        kk = jnp.concatenate([kg, kg], axis=1)
        for j in range(4):
            h = g * 4 + j
            rows = pl.ds(pl.multiple_of(h * HEAD_DIM, HEAD_DIM), HEAD_DIM)

            def place(part):
                pieces = []
                if j:
                    pieces.append(jnp.zeros((HEAD_DIM * j, count), BF16))
                pieces.append(part)
                if j < 3:
                    pieces.append(jnp.zeros((HEAD_DIM * (3 - j), count), BF16))
                return pieces

            qq = jnp.concatenate(place(qh_s[rows, :]) + place(ql_s[rows, :]), axis=0)
            s = jnp.dot(kk, qq, preferred_element_type=F32)
            sc = sc_s[pl.ds(h, 1), :]
            top = jnp.maximum(jnp.max(s, axis=0, keepdims=True), sc)
            weights = jnp.exp2(s - top).astype(BF16)
            pc = jnp.exp2(sc - top)
            vv = jnp.concatenate([vt_s[rows, :], ones], axis=0)
            o = jnp.dot(vv, weights, preferred_element_type=F32)
            total = o[HEAD_DIM : HEAD_DIM + 1] + pc
            summed = o[:HEAD_DIM] + widen(vc_s[rows, :]) * pc.astype(BF16).astype(F32)
            inner_s[rows, :] = (summed / total + widen(gl_s[rows, :])).astype(BF16)
        return carry

    lax.fori_loop(0, HEADS // 4, group, 0)
    tn = (((0,), (0,)), ((), ()))
    update = lax.dot_general(inner_s[...], wo_ref[...], tn, preferred_element_type=F32)
    out_ref[...] = update.astype(BF16).reshape(out_ref.shape)


def window_attention(grouped, aux, wk, wqt, wvt, wo):
    rows, tokens, width = grouped.shape
    cell = WIN * WIN
    count = rows * cell
    whole = pl.BlockSpec((width, width), lambda c: (0, 0))
    cube = pl.BlockSpec((rows, cell, width), lambda c: (0, c, 0))
    return pl.pallas_call(
        window_kernel,
        grid=(tokens // cell,),
        in_specs=[cube, pl.BlockSpec((1, 8, width), lambda c: (c, 0, 0)), whole, whole, whole, whole],
        out_specs=cube,
        out_shape=jax.ShapeDtypeStruct(grouped.shape, BF16),
        scratch_shapes=[
            pltpu.VMEM((count, width), BF16),
            pltpu.VMEM((width, count), BF16),
            pltpu.VMEM((width, count), BF16),
            pltpu.VMEM((width, count), BF16),
            pltpu.VMEM((HEADS, count), F32),
            pltpu.VMEM((width, 128), F32),
            pltpu.VMEM((width, 128), F32),
            pltpu.VMEM((width, count), BF16),
        ],
        compiler_params=pltpu.CompilerParams(vmem_limit_bytes=VMEM_LIMIT),
        cost_estimate=pl.CostEstimate(flops=20_000_000_000, bytes_accessed=4 << 20, transcendentals=8 << 20),
    )(grouped, aux, wk, wqt, wvt, wo)


def normalize(rows):
    dests, tokens, width = rows.shape
    steps = 2
    cells = dests * tokens // (WIN * WIN)
    return pl.pallas_call(
        norm_kernel,
        grid=(steps,),
        in_specs=[pl.BlockSpec((dests // steps, tokens, width), lambda i: (i, 0, 0))],
        out_specs=[
            pl.BlockSpec((dests // steps, tokens, width), lambda i: (i, 0, 0)),
            pl.BlockSpec((cells // steps, width), lambda i: (i, 0)),
        ],
        out_shape=[
            jax.ShapeDtypeStruct(rows.shape, BF16),
            jax.ShapeDtypeStruct((cells, width), F32),
        ],
        compiler_params=pltpu.CompilerParams(vmem_limit_bytes=VMEM_LIMIT),
        cost_estimate=pl.CostEstimate(flops=10_000_000, bytes_accessed=2 << 20, transcendentals=0),
    )(rows)


def carrier_tokens(sums):
    halves, rows, cells, width = sums.shape
    return pl.pallas_call(
        carrier_kernel,
        out_shape=jax.ShapeDtypeStruct((halves * cells, width), BF16),
        compiler_params=pltpu.CompilerParams(vmem_limit_bytes=VMEM_LIMIT),
        cost_estimate=pl.CostEstimate(flops=1_000_000, bytes_accessed=1 << 19, transcendentals=0),
    )(sums)


def glob_of(carriers, own, weights):
    return pl.pallas_call(
        glob_kernel,
        out_shape=jax.ShapeDtypeStruct((own.shape[0], 8, own.shape[1]), F32),
        compiler_params=pltpu.CompilerParams(vmem_limit_bytes=VMEM_LIMIT),
        cost_estimate=pl.CostEstimate(flops=300_000_000, bytes_accessed=2 << 20, transcendentals=16384),
    )(carriers, own, weights)


def body(tokens, weights, w_out):
    window = lax.axis_size("window")
    width = tokens.shape[-1]
    groups = [[h * WIN + l for l in range(WIN)] for h in range(window // WIN)]
    rows = tokens.reshape(WIN, -1, width)
    own_count = rows.shape[1] // (WIN * WIN)
    normed, sums = normalize(rows)
    grouped = lax.all_to_all(normed, "window", split_axis=0, concat_axis=0, tiled=True, axis_index_groups=groups)
    sums = lax.all_gather(sums, "window", axis=0)
    near = carrier_tokens(sums.reshape(window // WIN, WIN, sums.shape[1], width))
    own = lax.dynamic_slice_in_dim(near, lax.axis_index("window") * own_count, own_count, 0)
    carriers = lax.all_gather(near, "inline", axis=0, tiled=True)
    aux = glob_of(carriers, own, weights)
    wqt = weights[:, :EMBED_SPAN].T
    wk = weights[:, EMBED_SPAN : 2 * EMBED_SPAN]
    wvt = weights[:, 2 * EMBED_SPAN :].T
    update = window_attention(grouped, aux, wk, wqt, wvt, w_out)
    returned = lax.all_to_all(update, "window", split_axis=0, concat_axis=0, tiled=True, axis_index_groups=groups)
    return returned.reshape(tokens.shape)


def solution(mesh):
    return jax.shard_map(
        body,
        mesh=mesh,
        in_specs=(P(("replica", "inline", "window"), None, None, None), P(), P()),
        out_specs=P(("replica", "inline", "window"), None, None, None),
        check_vma=False,
    )
```

time: 555 us -> 194 us (0.35)
  the two profiles are of different devices: /device:TPU:32 before, /device:TPU:2 now
where the time goes in v1:
time: 194 us
  blocking collectives  148 us (76%)
  Pallas kernels  22.2 us (11%)
  starting transfers between devices  12.5 us (6%)
  local copies, waits for them, and re-layouts  10.8 us (6%)
    all_gather x1, blocking collectives, body(): sums = lax.all_gather(sums, 'window', axis=0)  70.1 us
    all_to_all x1, blocking collectives, body(): lax.all_to_all(update, 'window', split_axis=0, concat_axis=0, tiled=True,...  43.3 us
    all_gather x1, blocking collectives, body(): carriers = lax.all_gather(near, 'inline', axis=0, tiled=True)  35 us
    pallas_call x1, Pallas kernels, window_attention(): pl.pallas_call(window_kernel, grid=(tokens // cell,), in_specs=[cube, pl....  19.8 us
    all_to_all x1, starting transfers between devices, body(): lax.all_to_all(normed, 'window', split_axis=0, concat_axis=0, tiled=True,...  12.5 us
    unnamed x15, local copies, waits for them, and re-layouts  9.61 us
  transfers between devices with their start and end apart: 1, of which 0 were waited for; matrix products, arithmetic and copies ran while one was open for 2% of the time, Pallas kernels for 1%

profile of v1, /device:TPU:2, one launch (start us, length us, event | category | flops | bytes accessed | tf_op | source)
XLA Modules:
  0.0 194.0 jit_solution(12714839082752062919)
XLA Ops:
  0.0 0.0 copy-start.1
  0.0 1.2 copy-done.1
  1.2 0.0 copy-start
  1.2 0.9 shard_map.37
  2.1 0.0 copy-start.2
  2.1 1.0 copy-done.2
  3.1 12.5 %all-to-all-start = ((bf16[8,128,512]{2,1,0:T(8,128)(2,1)}), bf16[8,128,512]{2,1,0:T(8,128)(2,1)S(1)}, u32[]{:S(2)}, u32[]{:S(2)}) async-start(bf16[8,128,512]{2,1,0:T(8,128)(2,1)} %copy-done.2), calls=%async_computation | async-start | bytes 2097152 | tf_op jit(solution)/shard_map/all_to_all | solution.py:196
  15.6 0.0 copy-done
  15.6 1.2 fusion
  16.8 1.3 copy.7
  18.0 2.1 %copy.6 = bf16[512,512]{0,1:T(8,128)(2,1)} copy(bf16[512,512]{1,0:T(8,128)(2,1)} %get-tuple-element.10) | data formatting | bytes 1048576
  20.1 70.1 %all-gather = f32[256,512]{1,0:T(8,128)S(1)} all-gather(f32[16,512]{1,0:T(8,128)S(1)} %get-tuple-element.8), channel_id=2, replica_groups=mesh['inline'=8,'window'=16,'replica'=4] {'window'}, dimensions={0}, use_global_device_ids=true | all-gather | bytes 557056 | tf_op jit(solution)/shard_map/all_gather | solution.py:197
  90.2 0.2 shard_map.38
  90.5 35.0 %all_gather.11.all_ref = bf16[256,512]{1,0:T(8,128)(2,1)S(1)} all-gather(bf16[32,512]{1,0:T(8,128)(2,1)S(1)} %shard_map.38), channel_id=1, replica_groups=mesh['inline'=8,'window'=16,'replica'=4] {'inline'}, dimensions={0}, use_global_device_ids=true | all-gather | bytes 294912 | tf_op jit(solution)/shard_map/all_gather | solution.py:200
  125.5 1.4 shard_map.39.aux_ref
  126.8 0.0 all-to-all-done.x_ref
  126.9 0.0 copy-start.3
  126.9 1.0 copy-done.3
  127.9 0.0 copy-start.4
  127.9 1.0 copy-done.4
  128.9 0.0 copy-start.5
  128.9 1.0 copy-done.5
  130.0 19.8 %shard_map.40 = bf16[8,128,512]{2,1,0:T(8,128)(2,1)S(1)} custom-call(bf16[8,128,512]{2,1,0:T(8,128)(2,1)S(1)} %all-to-all-done.x_ref, f32[2,8,512]{2,1,0:T(8,128)S(1)} %shard_map.39.aux_ref, bf16[512,512]{1,0:T(8,128)(2,1)S(1)} %copy-done.4, bf16[512,512]{1,0:T(8,128)(2,1)S(1)} %bitcast.8, bf16[512,512]{1,0:T(8,128)(2,1)S(1)} %bitcast.7, ...), custom_call_target="tpu_custom_call" | custom-call | flops 20000000000 | bytes 4194304 | tf_op jit(solution)/shard_map/pallas_call | solution.py:128
  149.8 43.3 %all_to_all.10 = bf16[8,128,512]{2,1,0:T(8,128)(2,1)S(1)} all-to-all(bf16[8,128,512]{2,1,0:T(8,128)(2,1)S(1)} %shard_map.40), channel_id=1, replica_groups={{0,4,8,12,16,20,24,28},{32,36,40,44,48,52,56,60},{1,5,9,13,17,21,25,29}..., dimensions={0} | all-to-all | bytes 2097152 | tf_op jit(solution)/shard_map/all_to_all | solution.py:206
  193.0 1.0 copy.9
  (1 shorter events, 0.0 us)
Async XLA Ops:
  0.0 1.2 copy-start.1
  1.2 14.4 %copy-start = (bf16[512,1536]{1,0:T(8,128)(2,1)S(1)}, bf16[512,1536]{1,0:T(8,128)(2,1)}, u32[]{:S(2)}) copy-start(bf16[512,1536]{1,0:T(8,128)(2,1)} %w_ref.1) | copy-start | bytes 4718596
  2.1 1.0 copy-start.2
  3.1 123.8 %all-to-all-start = ((bf16[8,128,512]{2,1,0:T(8,128)(2,1)}), bf16[8,128,512]{2,1,0:T(8,128)(2,1)S(1)}, u32[]{:S(2)}, u32[]{:S(2)}) async-start(bf16[8,128,512]{2,1,0:T(8,128)(2,1)} %copy-done.2), calls=%async_computation | async-start | bytes 2097152 | tf_op jit(solution)/shard_map/all_to_all | solution.py:196
  126.9 1.0 copy-start.3
  127.9 1.0 copy-start.4
  128.9 1.0 copy-start.5

commit v2 on v1

v2 whole, which is shorter than its diff:
```python
import jax
import jax.numpy as jnp
from jax import lax
from jax.experimental import pallas as pl
from jax.experimental.pallas import tpu as pltpu
from jax.sharding import PartitionSpec as P

EMBED_SPAN = 512
HEADS = 16
HEAD_DIM = EMBED_SPAN // HEADS
WIN = 8
EPSILON = 1e-05
LOG2E = 1.4426950408889634
SCALE = HEAD_DIM ** (-0.5)
F32 = jnp.float32
BF16 = jnp.bfloat16
NT = (((1,), (1,)), ((), ()))
TN = (((0,), (0,)), ((), ()))
PARAMS = pltpu.CompilerParams(vmem_limit_bytes=32 * 1024 * 1024)


def cost(flops, size, transcendentals=0):
    return pl.CostEstimate(flops=flops, bytes_accessed=size, transcendentals=transcendentals)


def in_hbm(*arrays):
    return [pltpu.with_memory_space_constraint(a, pltpu.HBM) for a in arrays]


def standardize(values):
    center = values - jnp.mean(values, axis=-1, keepdims=True)
    spread = jnp.mean(center * center, axis=-1, keepdims=True)
    return center * lax.rsqrt(spread + EPSILON)


def norm_kernel(x_ref, wq_ref, wv_ref, normed_ref, wqt_ref, wvt_ref):
    normed_ref[...] = standardize(x_ref[...].astype(F32)).astype(BF16)

    @pl.when(pl.program_id(0) == 0)
    def _():
        row = lax.broadcasted_iota(jnp.int32, (EMBED_SPAN, EMBED_SPAN), 0)
        lane = lax.broadcasted_iota(jnp.int32, (EMBED_SPAN, EMBED_SPAN), 1)
        eye = jnp.where(row == lane, 1.0, 0.0).astype(BF16)
        wqt_ref[...] = lax.dot_general(eye, wq_ref[...], NT, preferred_element_type=F32).astype(BF16)
        wvt_ref[...] = lax.dot_general(eye, wv_ref[...], NT, preferred_element_type=F32).astype(BF16)


def normalize(rows, weights):
    dests, tokens, width = rows.shape
    steps = 4
    block = pl.BlockSpec((dests // steps, tokens, width), lambda i: (i, 0, 0))
    square = pltpu.HBM((width, width), BF16)
    whole = pl.BlockSpec((width, width), lambda i: (0, 0))
    rows, weights = in_hbm(rows, weights)
    return pl.pallas_call(
        norm_kernel,
        grid=(steps,),
        in_specs=[block, whole, pl.BlockSpec((width, width), lambda i: (0, 2))],
        out_specs=[block, whole, whole],
        out_shape=[jax.ShapeDtypeStruct(rows.shape, BF16), square, square],
        compiler_params=PARAMS,
        cost_estimate=cost(600_000_000, 4 << 20),
    )(rows, weights, weights)


def carrier_kernel(x_ref, out_ref, copies_ref):
    rows, tokens, width = x_ref.shape
    cell = WIN * WIN
    own = []
    for c in range(tokens // cell):
        cube = x_ref[:, c * cell : (c + 1) * cell, :].astype(F32)
        mean = jnp.sum(jnp.sum(cube, axis=0), axis=0, keepdims=True) * (1.0 / (rows * cell))
        own.append(standardize(mean))
        out_ref[c] = jnp.broadcast_to(own[-1].astype(BF16).astype(F32), (8, width))
    copies_ref[...] = jnp.broadcast_to(jnp.concatenate(own, axis=0)[None], copies_ref.shape).astype(BF16)


def own_carriers(grouped, window):
    rows, tokens, width = grouped.shape
    own_count = tokens // (WIN * WIN)
    return pl.pallas_call(
        carrier_kernel,
        out_shape=[jax.ShapeDtypeStruct((own_count, 8, width), F32), jax.ShapeDtypeStruct((window, own_count, width), BF16)],
        compiler_params=PARAMS,
        cost_estimate=cost(1_000_000, 1 << 20),
    )(grouped)


def head_mask(rows):
    lane = lax.broadcasted_iota(jnp.int32, (rows, EMBED_SPAN), 1) // HEAD_DIM
    row = lax.broadcasted_iota(jnp.int32, (rows, EMBED_SPAN), 0) % HEADS
    return lane == row


def window_kernel(x_ref, car_ref, wk_ref, wqt_ref, wvt_ref, out_ref, k_s, qh_s, ql_s, vt_s, sc_s, vc_s):
    count = WIN**3
    x = x_ref[...].reshape(count, EMBED_SPAN)
    k_s[...] = jnp.dot(x, wk_ref[...], preferred_element_type=F32).astype(BF16)
    q = lax.dot_general(wqt_ref[...], x, NT, preferred_element_type=F32).astype(BF16).astype(F32) * (SCALE * LOG2E)
    high = q.astype(BF16)
    low = (q - high.astype(F32)).astype(BF16)
    qh_s[...] = high
    ql_s[...] = low
    vt_s[...] = lax.dot_general(wvt_ref[...], x, NT, preferred_element_type=F32).astype(BF16)
    carrier = jnp.broadcast_to(car_ref[0, 0:1, :], (128, EMBED_SPAN)).astype(BF16)
    kc = jnp.dot(carrier[:16], wk_ref[...], preferred_element_type=F32)
    kc = jnp.where(head_mask(HEADS), kc, 0.0).astype(BF16)
    sc_s[...] = jnp.dot(kc, high, preferred_element_type=F32) + jnp.dot(kc, low, preferred_element_type=F32)
    vc_s[...] = lax.dot_general(wvt_ref[...], carrier, NT, preferred_element_type=F32).astype(BF16).astype(F32)
    ones = jnp.ones((16, count), BF16)

    def scores(h):
        group, j = h // 4, h % 4
        keys = k_s[:, group * 128 : (group + 1) * 128]
        rows = slice(h * HEAD_DIM, (h + 1) * HEAD_DIM)
        before = [jnp.zeros((HEAD_DIM * j, count), BF16)] if j else []
        after = [jnp.zeros((HEAD_DIM * (3 - j), count), BF16)] if j < 3 else []
        queries = before + [qh_s[rows, :]] + after + before + [ql_s[rows, :]] + after
        return jnp.dot(jnp.concatenate([keys, keys], axis=1), jnp.concatenate(queries, axis=0), preferred_element_type=F32)

    def mix(h, s):
        rows = slice(h * HEAD_DIM, (h + 1) * HEAD_DIM)
        sc = sc_s[h : h + 1, :]
        top = jnp.maximum(jnp.max(s, axis=0, keepdims=True), sc)
        weights = jnp.exp2(s - top).astype(BF16)
        pc = jnp.exp2(sc - top)
        values = jnp.concatenate([vt_s[rows, :], ones], axis=0)
        o = jnp.dot(values, weights, preferred_element_type=F32)
        total = o[HEAD_DIM : HEAD_DIM + 1] + pc
        column = jnp.concatenate([vc_s[rows, :]] * (count // 128), axis=1)
        out_ref[rows, :] = (o[:HEAD_DIM] + column * pc.astype(BF16).astype(F32)) / total

    ahead = []
    for h in range(HEADS):
        ahead.append((h, scores(h)))
        if len(ahead) > 2:
            mix(*ahead.pop(0))
    for item in ahead:
        mix(*item)


def window_attention(grouped, own, c, weights, wqt, wvt):
    rows, tokens, width = grouped.shape
    cell = WIN * WIN
    count = rows * cell
    whole = pl.BlockSpec((width, width), lambda i: (0, 0))
    half = pltpu.VMEM((width, count), BF16)
    weights, wqt, wvt = in_hbm(weights, wqt, wvt)
    return pl.pallas_call(
        window_kernel,
        grid=(1,),
        in_specs=[
            pl.BlockSpec((rows, cell, width), lambda i: (0, c, 0)),
            pl.BlockSpec((1, 8, width), lambda i: (c, 0, 0)),
            pl.BlockSpec((width, width), lambda i: (0, 1)),
            whole,
            whole,
        ],
        out_specs=pl.BlockSpec((width, count), lambda i: (0, 0)),
        out_shape=pltpu.HBM((width, count), F32),
        scratch_shapes=[pltpu.VMEM((count, width), BF16), half, half, half, pltpu.VMEM((HEADS, count), F32), pltpu.VMEM((width, 128), F32)],
        compiler_params=PARAMS,
        cost_estimate=cost(8_000_000_000, 4 << 20, 4 << 20),
    )(grouped, own, weights, wqt, wvt)


def glob_kernel(all_ref, own_ref, w_ref, wo_ref, *rest):
    out_ref = rest[-1]
    match = jnp.dot(all_ref[...], w_ref[:, EMBED_SPAN:], preferred_element_type=F32).astype(BF16)
    keys, values = match[:, :EMBED_SPAN], match[:, EMBED_SPAN:]
    mask = head_mask(HEADS)
    cell = WIN * WIN
    for c, local_ref in enumerate(rest[:-1]):
        own = jnp.broadcast_to(own_ref[c, 0:1, :], (16, EMBED_SPAN)).astype(BF16)
        queries = jnp.dot(own, w_ref[:, :EMBED_SPAN], preferred_element_type=F32)
        queries = jnp.where(mask, queries, 0.0).astype(BF16)
        s = lax.dot_general(queries, keys, NT, preferred_element_type=F32) * SCALE
        weights = jnp.exp(s - jnp.max(s, axis=-1, keepdims=True))
        total = jnp.sum(weights, axis=-1, keepdims=True)
        summed = jnp.dot(weights.astype(BF16), values, preferred_element_type=F32) / total
        glob = jnp.sum(jnp.where(mask, summed, 0.0), axis=0, keepdims=True)
        column = jnp.broadcast_to(glob, (128, EMBED_SPAN)).T
        column = jnp.concatenate([column] * (local_ref.shape[1] // 128), axis=1)
        inner = (local_ref[...] + column).astype(BF16)
        update = lax.dot_general(inner, wo_ref[...], TN, preferred_element_type=F32).astype(BF16)
        out_ref[:, c * cell : (c + 1) * cell, :] = update.reshape(-1, cell, EMBED_SPAN)


def finish(carriers, own, weights, w_out, local, shape):
    return pl.pallas_call(
        glob_kernel,
        out_shape=jax.ShapeDtypeStruct(shape, BF16),
        compiler_params=PARAMS,
        cost_estimate=cost(1_000_000_000, 6 << 20, 16384),
    )(carriers, own, weights, w_out, *in_hbm(*local))


def exchange(values, axis, groups=None):
    return lax.all_to_all(values, axis, split_axis=0, concat_axis=0, tiled=True, axis_index_groups=groups)


def spread(values, axis):
    return exchange(jnp.broadcast_to(values[None], (lax.axis_size(axis),) + values.shape), axis)


def body(tokens, weights, w_out):
    window = lax.axis_size("window")
    width = tokens.shape[-1]
    groups = [[h * WIN + l for l in range(WIN)] for h in range(window // WIN)]
    rows = tokens.reshape(WIN, -1, width)
    normed, wqt, wvt = normalize(rows, weights)
    grouped = exchange(normed, "window", groups)
    own, copies = own_carriers(grouped, window)
    near = exchange(copies, "window").reshape(-1, width)
    first = window_attention(grouped, own, 0, weights, wqt, wvt)
    grouped, near = lax.optimization_barrier((grouped, near))
    carriers = spread(near, "inline").reshape(-1, width)
    second = window_attention(grouped, own, 1, weights, wqt, wvt)
    update = finish(carriers, own, weights, w_out, (first, second), grouped.shape)
    return exchange(update, "window", groups).reshape(tokens.shape)


def solution(mesh):
    return jax.shard_map(
        body,
        mesh=mesh,
        in_specs=(P(("replica", "inline", "window"), None, None, None), P(), P()),
        out_specs=P(("replica", "inline", "window"), None, None, None),
        check_vma=False,
    )
```

time: 194 us -> 165 us (0.85)
  the two profiles are of different devices: /device:TPU:2 before, /device:TPU:1 now
where the time goes in v2:
time: 165 us; the launch traced here: 164 us
  blocking collectives  118 us (72%)
  Pallas kernels  25.8 us (16%)
  starting transfers between devices  14.1 us (9%)
  waiting for transfers between devices  3.52 us (2%)
  local copies, waits for them, and re-layouts  1.72 us (1%)
    all_to_all x2, blocking collectives, exchange(): lax.all_to_all(values, axis, split_axis=0, concat_axis=0, tiled=True, axi...  118 us
    pallas_call x2, Pallas kernels, window_attention(): pl.pallas_call(window_kernel, grid=(1,), in_specs=[pl.BlockSpec((rows, ce...  16 us
    all_to_all x2, starting transfers between devices, exchange(): lax.all_to_all(values, axis, split_axis=0, concat_axis=0, tiled=True, axi...  14.1 us
    pallas_call x1, Pallas kernels, normalize(): pl.pallas_call(norm_kernel, grid=(steps,), in_specs=[block, whole, pl.Blo...  4.79 us
    pallas_call x1, Pallas kernels, finish(): pl.pallas_call(glob_kernel, out_shape=jax.ShapeDtypeStruct(shape, BF16),...  3.99 us
    all_to_all x2, waiting for transfers between devices, exchange(): lax.all_to_all(values, axis, split_axis=0, concat_axis=0, tiled=True, axi...  3.52 us
  transfers between devices with their start and end apart: 2, of which 1 were waited for; matrix products, arithmetic and copies ran while one was open for 0% of the time, Pallas kernels for 10%

profile of v2, /device:TPU:1, one launch (start us, length us, event | category | flops | bytes accessed | tf_op | source)
XLA Modules:
  0.0 163.6 jit_solution(17793513070486863860)
XLA Ops:
  0.0 4.8 %shard_map.37 = (bf16[8,128,512]{2,1,0:T(8,128)(2,1)S(1)}, bf16[512,512]{1,0:T(8,128)(2,1)}, bf16[512,512]{1,0:T(8,128)(2,1)}) custom-call(bf16[8,128,512]{2,1,0:T(8,128)(2,1)} %bitcast.5, bf16[512,1536]{1,0:T(8,128)(2,1)} %w_ref.1, bf16[512,1536]{1,0:T(8,128)(2,1)} %w_ref.1), custom_call_target="tpu_custom_call" | custom-call | flops 600000000 | bytes 4194304 | tf_op jit(solution)/shard_map/pallas_call | solution.py:55
  4.8 63.2 %all_to_all.20.x_ref = bf16[8,128,512]{2,1,0:T(8,128)(2,1)S(1)} all-to-all(bf16[8,128,512]{2,1,0:T(8,128)(2,1)S(1)} %get-tuple-element.12), channel_id=1, replica_groups={{0,4,8,12,16,20,24,28},{32,36,40,44,48,52,56,60},{1,5,9,13,17,21,25,29}..., dimensions={0} | all-to-all | bytes 2097152 | tf_op jit(solution)/shard_map/all_to_all | solution.py:199
  68.0 1.0 shard_map.38
  69.0 7.4 %all-to-all-start.1 = ((bf16[16,2,512]{2,1,0:T(2,128)(2,1)}), bf16[16,2,512]{2,1,0:T(2,128)(2,1)S(1)}, u32[]{:S(2)}, u32[]{:S(2)}) async-start(bf16[16,2,512]{2,1,0:T(2,128)(2,1)} %get-tuple-element.13), calls=%async_computation.1 | async-start | bytes 65536 | tf_op jit(solution)/shard_map/all_to_all | solution.py:199
  76.4 8.0 %shard_map.39.rest_0_ = f32[512,512]{1,0:T(8,128)} custom-call(bf16[8,128,512]{2,1,0:T(8,128)(2,1)S(1)} %all_to_all.20.x_ref, f32[2,8,512]{2,1,0:T(8,128)S(1)} %get-tuple-element.15.car_ref.own_ref, bf16[512,1536]{1,0:T(8,128)(2,1)} %w_ref.1, bf16[512,512]{1,0:T(8,128)(2,1)} %get-tuple-element.16.wqt_ref, bf16[512,512]{1,0:T(8,128)(2,1)} %get-tuple-element.17.wvt_ref), custom_call_target="tpu_custom_call" | custom-call | flops 8000000000 | bytes 4194304 | tf_op jit(solution)/shard_map/pallas_call | solution.py:149
  84.3 3.5 %all-to-all-done.1 = bf16[16,2,512]{2,1,0:T(2,128)(2,1)S(1)} async-done(((bf16[16,2,512]{2,1,0:T(2,128)(2,1)}), bf16[16,2,512]{2,1,0:T(2,128)(2,1)S(1)}, u32[]{:S(2)}, u32[]{:S(2)}) %all-to-all-start.1) | async-done | bytes 32800 | tf_op jit(solution)/shard_map/all_to_all | solution.py:199
  87.9 0.7 broadcast_in_dim.2
  88.6 6.7 %all-to-all-start.2 = ((bf16[8,32,512]{2,1,0:T(8,128)(2,1)}), bf16[8,32,512]{2,1,0:T(8,128)(2,1)S(1)}, u32[]{:S(2)}, u32[]{:S(2)}) async-start(bf16[8,32,512]{2,1,0:T(8,128)(2,1)} %broadcast_in_dim.2), calls=%async_computation.2 | async-start | bytes 524288 | tf_op jit(solution)/shard_map/all_to_all | solution.py:199
  95.3 0.0 copy-start
  95.3 0.0 copy-start.1
  95.3 8.1 %shard_map.40.rest_1_ = f32[512,512]{1,0:T(8,128)} custom-call(bf16[8,128,512]{2,1,0:T(8,128)(2,1)S(1)} %all_to_all.20.x_ref, f32[2,8,512]{2,1,0:T(8,128)S(1)} %get-tuple-element.15.car_ref.own_ref, bf16[512,1536]{1,0:T(8,128)(2,1)} %w_ref.1, bf16[512,512]{1,0:T(8,128)(2,1)} %get-tuple-element.16.wqt_ref, bf16[512,512]{1,0:T(8,128)(2,1)} %get-tuple-element.17.wvt_ref), custom_call_target="tpu_custom_call" | custom-call | flops 8000000000 | bytes 4194304 | tf_op jit(solution)/shard_map/pallas_call | solution.py:149
  103.4 0.0 all-to-all-done.2
  103.4 0.0 copy-done
  103.4 0.0 copy-done.1
  103.4 4.0 %shard_map.41 = bf16[8,128,512]{2,1,0:T(8,128)(2,1)S(1)} custom-call(bf16[256,512]{1,0:T(8,128)(2,1)S(1)} %bitcast.3, f32[2,8,512]{2,1,0:T(8,128)S(1)} %get-tuple-element.15.car_ref.own_ref, bf16[512,1536]{1,0:T(8,128)(2,1)S(1)} %copy-done, bf16[512,512]{1,0:T(8,128)(2,1)S(1)} %copy-done.1, f32[512,512]{1,0:T(8,128)} %shard_map.39.rest_0_, ...), custom_call_target="tpu_custom_call" | custom-call | flops 1000000000 | bytes 6291456 | tf_op jit(solution)/shard_map/pallas_call | solution.py:190
  107.4 55.2 %all_to_all.21 = bf16[8,128,512]{2,1,0:T(8,128)(2,1)S(1)} all-to-all(bf16[8,128,512]{2,1,0:T(8,128)(2,1)S(1)} %shard_map.41), channel_id=1, replica_groups={{0,4,8,12,16,20,24,28},{32,36,40,44,48,52,56,60},{1,5,9,13,17,21,25,29}..., dimensions={0} | all-to-all | bytes 2097152 | tf_op jit(solution)/shard_map/all_to_all | solution.py:199
  162.6 1.0 copy.5
  (1 shorter events, 0.0 us)
Async XLA Ops:
  69.0 18.9 %all-to-all-start.1 = ((bf16[16,2,512]{2,1,0:T(2,128)(2,1)}), bf16[16,2,512]{2,1,0:T(2,128)(2,1)S(1)}, u32[]{:S(2)}, u32[]{:S(2)}) async-start(bf16[16,2,512]{2,1,0:T(2,128)(2,1)} %get-tuple-element.13), calls=%async_computation.1 | async-start | bytes 65536 | tf_op jit(solution)/shard_map/all_to_all | solution.py:199
  88.6 14.8 %all-to-all-start.2 = ((bf16[8,32,512]{2,1,0:T(8,128)(2,1)}), bf16[8,32,512]{2,1,0:T(8,128)(2,1)S(1)}, u32[]{:S(2)}, u32[]{:S(2)}) async-start(bf16[8,32,512]{2,1,0:T(8,128)(2,1)} %broadcast_in_dim.2), calls=%async_computation.2 | async-start | bytes 524288 | tf_op jit(solution)/shard_map/all_to_all | solution.py:199
  95.3 8.1 %copy-start = (bf16[512,1536]{1,0:T(8,128)(2,1)S(1)}, bf16[512,1536]{1,0:T(8,128)(2,1)}, u32[]{:S(2)}) copy-start(bf16[512,1536]{1,0:T(8,128)(2,1)} %w_ref.1) | copy-start | bytes 4718596
  95.3 8.1 %copy-start.1 = (bf16[512,512]{1,0:T(8,128)(2,1)S(1)}, bf16[512,512]{1,0:T(8,128)(2,1)}, u32[]{:S(2)}) copy-start(bf16[512,512]{1,0:T(8,128)(2,1)} %wo_ref.1) | copy-start | bytes 1572868

commit v3 on v2

v3 whole, which is shorter than its diff:
```python
import jax
import jax.numpy as jnp
from jax import lax
from jax.experimental import pallas as pl
from jax.experimental.pallas import tpu as pltpu
from jax.sharding import PartitionSpec as P

EMBED_SPAN = 512
HEADS = 16
HEAD_DIM = EMBED_SPAN // HEADS
WIN = 8
EPSILON = 1e-05
LOG2E = 1.4426950408889634
SCALE = HEAD_DIM ** (-0.5)
F32 = jnp.float32
BF16 = jnp.bfloat16
NT = (((1,), (1,)), ((), ()))
TN = (((0,), (0,)), ((), ()))
PARAMS = pltpu.CompilerParams(vmem_limit_bytes=32 * 1024 * 1024)


def cost(flops, size, transcendentals=0):
    return pl.CostEstimate(flops=flops, bytes_accessed=size, transcendentals=transcendentals)


def in_hbm(*arrays):
    return [pltpu.with_memory_space_constraint(a, pltpu.HBM) for a in arrays]


def standardize(values):
    center = values - jnp.mean(values, axis=-1, keepdims=True)
    spread = jnp.mean(center * center, axis=-1, keepdims=True)
    return center * lax.rsqrt(spread + EPSILON)


def norm_kernel(x_ref, normed_ref, sums_ref):
    dests, tokens, width = x_ref.shape
    cell = WIN * WIN
    normed = standardize(x_ref[...].astype(F32)).astype(BF16)
    normed_ref[...] = normed
    sums_ref[...] = jnp.sum(normed.astype(F32).reshape(dests, tokens // cell, cell, width), axis=2)


def normalize(rows):
    dests, tokens, width = rows.shape
    steps = 4
    cells = tokens // (WIN * WIN)
    block = pl.BlockSpec((dests // steps, tokens, width), lambda i: (i, 0, 0))
    return pl.pallas_call(
        norm_kernel,
        grid=(steps,),
        in_specs=[block],
        out_specs=[block, pl.BlockSpec((dests // steps, cells, width), lambda i: (i, 0, 0))],
        out_shape=[jax.ShapeDtypeStruct(rows.shape, BF16), jax.ShapeDtypeStruct((dests, cells, width), F32)],
        compiler_params=PARAMS,
        cost_estimate=cost(10_000_000, 2 << 20),
    )(*in_hbm(rows))


def turn_kernel(wq_ref, wv_ref, wqt_ref, wvt_ref):
    row = lax.broadcasted_iota(jnp.int32, (EMBED_SPAN, EMBED_SPAN), 0)
    lane = lax.broadcasted_iota(jnp.int32, (EMBED_SPAN, EMBED_SPAN), 1)
    eye = jnp.where(row == lane, 1.0, 0.0).astype(BF16)
    wqt_ref[...] = lax.dot_general(eye, wq_ref[...], NT, preferred_element_type=F32).astype(BF16)
    wvt_ref[...] = lax.dot_general(eye, wv_ref[...], NT, preferred_element_type=F32).astype(BF16)


def turn(weights):
    width = weights.shape[0]
    square = pltpu.HBM((width, width), BF16)
    whole = pl.BlockSpec((width, width), lambda i: (0, 0))
    (weights,) = in_hbm(weights)
    return pl.pallas_call(
        turn_kernel,
        grid=(1,),
        in_specs=[whole, pl.BlockSpec((width, width), lambda i: (0, 2))],
        out_specs=[whole, whole],
        out_shape=[square, square],
        compiler_params=PARAMS,
        cost_estimate=cost(600_000_000, 2 << 20),
    )(weights, weights)


def carrier_kernel(x_ref, out_ref, copies_ref):
    own_count, rows, width = out_ref.shape
    tokens = x_ref.shape[1] // own_count
    own = []
    for c in range(own_count):
        cube = x_ref[:, c * tokens : (c + 1) * tokens, :].astype(F32)
        mean = jnp.sum(jnp.sum(cube, axis=0), axis=0, keepdims=True) * (1.0 / WIN**3)
        own.append(standardize(mean))
        out_ref[c] = jnp.broadcast_to(own[-1].astype(BF16).astype(F32), (rows, width))
    copies_ref[...] = jnp.broadcast_to(jnp.concatenate(own, axis=0)[None], copies_ref.shape).astype(BF16)


def own_carriers(values, own_count, window):
    width = values.shape[-1]
    return pl.pallas_call(
        carrier_kernel,
        out_shape=[jax.ShapeDtypeStruct((own_count, 8, width), F32), jax.ShapeDtypeStruct((window, own_count, width), BF16)],
        compiler_params=PARAMS,
        cost_estimate=cost(1_000_000, 1 << 20),
    )(values)


def head_mask(rows):
    lane = lax.broadcasted_iota(jnp.int32, (rows, EMBED_SPAN), 1) // HEAD_DIM
    row = lax.broadcasted_iota(jnp.int32, (rows, EMBED_SPAN), 0) % HEADS
    return lane == row


def widen(column, count):
    return jnp.concatenate([column] * (count // 128), axis=1)


def attend(x_ref, car_ref, wk_ref, wqt_ref, wvt_ref, k_s, qh_s, ql_s, vt_s, sc_s, vc_s, write):
    count = WIN**3
    x = x_ref[...].reshape(count, EMBED_SPAN)
    k_s[...] = jnp.dot(x, wk_ref[...], preferred_element_type=F32).astype(BF16)
    q = lax.dot_general(wqt_ref[...], x, NT, preferred_element_type=F32).astype(BF16).astype(F32) * (SCALE * LOG2E)
    high = q.astype(BF16)
    low = (q - high.astype(F32)).astype(BF16)
    qh_s[...] = high
    ql_s[...] = low
    vt_s[...] = lax.dot_general(wvt_ref[...], x, NT, preferred_element_type=F32).astype(BF16)
    carrier = jnp.broadcast_to(car_ref[0, 0:1, :], (128, EMBED_SPAN)).astype(BF16)
    kc = jnp.dot(carrier[:16], wk_ref[...], preferred_element_type=F32)
    kc = jnp.where(head_mask(HEADS), kc, 0.0).astype(BF16)
    sc_s[...] = jnp.dot(kc, high, preferred_element_type=F32) + jnp.dot(kc, low, preferred_element_type=F32)
    vc_s[...] = lax.dot_general(wvt_ref[...], carrier, NT, preferred_element_type=F32).astype(BF16).astype(F32)
    ones = jnp.ones((16, count), BF16)

    def scores(h):
        group, j = h // 4, h % 4
        keys = k_s[:, group * 128 : (group + 1) * 128]
        rows = slice(h * HEAD_DIM, (h + 1) * HEAD_DIM)
        before = [jnp.zeros((HEAD_DIM * j, count), BF16)] if j else []
        after = [jnp.zeros((HEAD_DIM * (3 - j), count), BF16)] if j < 3 else []
        queries = before + [qh_s[rows, :]] + after + before + [ql_s[rows, :]] + after
        return jnp.dot(jnp.concatenate([keys, keys], axis=1), jnp.concatenate(queries, axis=0), preferred_element_type=F32)

    def mix(h, s):
        rows = slice(h * HEAD_DIM, (h + 1) * HEAD_DIM)
        sc = sc_s[h : h + 1, :]
        top = jnp.maximum(jnp.max(s, axis=0, keepdims=True), sc)
        weights = jnp.exp2(s - top).astype(BF16)
        pc = jnp.exp2(sc - top)
        values = jnp.concatenate([vt_s[rows, :], ones], axis=0)
        o = jnp.dot(values, weights, preferred_element_type=F32)
        total = o[HEAD_DIM : HEAD_DIM + 1] + pc
        write(rows, (o[:HEAD_DIM] + widen(vc_s[rows, :], count) * pc.astype(BF16).astype(F32)) / total)

    ahead = []
    for h in range(HEADS):
        ahead.append((h, scores(h)))
        if len(ahead) > 2:
            mix(*ahead.pop(0))
    for item in ahead:
        mix(*item)


def attend_scratch():
    count = WIN**3
    half = pltpu.VMEM((EMBED_SPAN, count), BF16)
    return [pltpu.VMEM((count, EMBED_SPAN), BF16), half, half, half, pltpu.VMEM((HEADS, count), F32), pltpu.VMEM((EMBED_SPAN, 128), F32)]


def local_kernel(x_ref, car_ref, wk_ref, wqt_ref, wvt_ref, out_ref, *scratch):
    def write(rows, local):
        out_ref[rows, :] = local

    attend(x_ref, car_ref, wk_ref, wqt_ref, wvt_ref, *scratch, write)


def local_attention(grouped, own, c, weights, wqt, wvt):
    rows, tokens, width = grouped.shape
    cell = WIN * WIN
    count = rows * cell
    whole = pl.BlockSpec((width, width), lambda i: (0, 0))
    weights, wqt, wvt = in_hbm(weights, wqt, wvt)
    return pl.pallas_call(
        local_kernel,
        grid=(1,),
        in_specs=[
            pl.BlockSpec((rows, cell, width), lambda i: (0, c, 0)),
            pl.BlockSpec((1, 8, width), lambda i: (c, 0, 0)),
            pl.BlockSpec((width, width), lambda i: (0, 1)),
            whole,
            whole,
        ],
        out_specs=pl.BlockSpec((width, count), lambda i: (0, 0)),
        out_shape=pltpu.HBM((width, count), F32),
        scratch_shapes=attend_scratch(),
        compiler_params=PARAMS,
        cost_estimate=cost(8_000_000_000, 4 << 20, 4 << 20),
    )(grouped, own, weights, wqt, wvt)


def whole_kernel(x_ref, car_ref, glob_ref, wk_ref, wqt_ref, wvt_ref, wo_ref, out_ref, inner_s, gl_s, *scratch):
    gl_s[...] = jnp.broadcast_to(glob_ref[0, 0:1, :], (128, EMBED_SPAN)).T

    def write(rows, local):
        inner_s[rows, :] = (local + widen(gl_s[rows, :], local.shape[1])).astype(BF16)

    attend(x_ref, car_ref, wk_ref, wqt_ref, wvt_ref, *scratch, write)
    update = lax.dot_general(inner_s[...], wo_ref[...], TN, preferred_element_type=F32)
    out_ref[...] = update.astype(BF16).reshape(out_ref.shape)


def whole_attention(grouped, own, glob, weights, wqt, wvt, w_out):
    rows, tokens, width = grouped.shape
    cell = WIN * WIN
    count = rows * cell
    cube = pl.BlockSpec((rows, cell, width), lambda i: (0, i, 0))
    row = pl.BlockSpec((1, 8, width), lambda i: (i, 0, 0))
    whole = pl.BlockSpec((width, width), lambda i: (0, 0))
    return pl.pallas_call(
        whole_kernel,
        grid=(tokens // cell,),
        in_specs=[cube, row, row, pl.BlockSpec((width, width), lambda i: (0, 1)), whole, whole, whole],
        out_specs=cube,
        out_shape=jax.ShapeDtypeStruct(grouped.shape, BF16),
        scratch_shapes=[pltpu.VMEM((width, count), BF16), pltpu.VMEM((width, 128), F32)] + attend_scratch(),
        compiler_params=PARAMS,
        cost_estimate=cost(17_000_000_000, 6 << 20, 8 << 20),
    )(grouped, own, glob, *in_hbm(weights, wqt, wvt, w_out))


def carrier_match(all_ref, w_ref):
    match = jnp.dot(all_ref[...], w_ref[:, EMBED_SPAN:], preferred_element_type=F32).astype(BF16)
    return match[:, :EMBED_SPAN], match[:, EMBED_SPAN:]


def carrier_attention(own, w_ref, keys, values):
    mask = head_mask(HEADS)
    own = jnp.broadcast_to(own, (16, EMBED_SPAN)).astype(BF16)
    queries = jnp.dot(own, w_ref[:, :EMBED_SPAN], preferred_element_type=F32)
    queries = jnp.where(mask, queries, 0.0).astype(BF16)
    s = lax.dot_general(queries, keys, NT, preferred_element_type=F32) * SCALE
    weights = jnp.exp(s - jnp.max(s, axis=-1, keepdims=True))
    total = jnp.sum(weights, axis=-1, keepdims=True)
    summed = jnp.dot(weights.astype(BF16), values, preferred_element_type=F32) / total
    return jnp.sum(jnp.where(mask, summed, 0.0), axis=0, keepdims=True)


def glob_kernel(all_ref, own_ref, w_ref, out_ref):
    keys, values = carrier_match(all_ref, w_ref)
    for c in range(out_ref.shape[0]):
        out_ref[c] = jnp.broadcast_to(carrier_attention(own_ref[c, 0:1, :], w_ref, keys, values), out_ref.shape[1:])


def glob_of(carriers, own, weights):
    return pl.pallas_call(
        glob_kernel,
        out_shape=jax.ShapeDtypeStruct(own.shape, F32),
        compiler_params=PARAMS,
        cost_estimate=cost(400_000_000, 2 << 20, 16384),
    )(carriers, own, weights)


def finish_kernel(all_ref, own_ref, w_ref, wo_ref, *rest):
    out_ref = rest[-1]
    keys, values = carrier_match(all_ref, w_ref)
    cell = WIN * WIN
    for c, local_ref in enumerate(rest[:-1]):
        glob = carrier_attention(own_ref[c, 0:1, :], w_ref, keys, values)
        column = widen(jnp.broadcast_to(glob, (128, EMBED_SPAN)).T, local_ref.shape[1])
        inner = (local_ref[...] + column).astype(BF16)
        update = lax.dot_general(inner, wo_ref[...], TN, preferred_element_type=F32).astype(BF16)
        out_ref[:, c * cell : (c + 1) * cell, :] = update.reshape(-1, cell, EMBED_SPAN)


def finish(carriers, own, weights, w_out, local, shape):
    return pl.pallas_call(
        finish_kernel,
        out_shape=jax.ShapeDtypeStruct(shape, BF16),
        compiler_params=PARAMS,
        cost_estimate=cost(1_000_000_000, 6 << 20, 16384),
    )(carriers, own, weights, w_out, *in_hbm(*local))


def exchange(values, axis, groups=None):
    return lax.all_to_all(values, axis, split_axis=0, concat_axis=0, tiled=True, axis_index_groups=groups)


def spread(values, axis):
    return exchange(jnp.broadcast_to(values[None], (lax.axis_size(axis),) + values.shape), axis)


def slab_first(normed, sums, weights, w_out, groups, window):
    width = normed.shape[-1]
    grouped = exchange(normed, "window", groups)
    own, copies = own_carriers(grouped, sums.shape[1], window)
    wqt, wvt = turn(weights)
    near = exchange(copies, "window").reshape(-1, width)
    first = local_attention(grouped, own, 0, weights, wqt, wvt)
    grouped, near = lax.optimization_barrier((grouped, near))
    carriers = spread(near, "inline").reshape(-1, width)
    second = local_attention(grouped, own, 1, weights, wqt, wvt)
    return finish(carriers, own, weights, w_out, (first, second), grouped.shape)


def carriers_first(normed, sums, weights, w_out, groups, window):
    width = normed.shape[-1]
    own, copies = own_carriers(exchange(sums, "window", groups), sums.shape[1], window)
    near = exchange(copies, "window").reshape(-1, width)
    carriers = spread(near, "inline").reshape(-1, width)
    normed, carriers = lax.optimization_barrier((normed, carriers))
    grouped = exchange(normed, "window", groups)
    wqt, wvt = turn(weights)
    glob = glob_of(carriers, own, weights)
    return whole_attention(grouped, own, glob, weights, wqt, wvt, w_out)


def body(tokens, weights, w_out):
    window = lax.axis_size("window")
    width = tokens.shape[-1]
    groups = [[h * WIN + l for l in range(WIN)] for h in range(window // WIN)]
    rows = tokens.reshape(WIN, -1, width)
    normed, sums = normalize(rows)
    update = lax.cond(
        lax.axis_index("replica") % 2 == 0,
        lambda *args: slab_first(*args, groups, window),
        lambda *args: carriers_first(*args, groups, window),
        normed, sums, weights, w_out,
    )
    return exchange(update, "window", groups).reshape(tokens.shape)


def solution(mesh):
    return jax.shard_map(
        body,
        mesh=mesh,
        in_specs=(P(("replica", "inline", "window"), None, None, None), P(), P()),
        out_specs=P(("replica", "inline", "window"), None, None, None),
        check_vma=False,
    )
```

time: 165 us -> 150 us (0.909)
  waiting for transfers between devices: 3.52 us -> 24.8 us
  blocking collectives: 118 us -> 98 us
  starting transfers between devices: 14.1 us -> 3.59 us
  Pallas kernels: 25.8 us -> 22.5 us
    all_to_all x2 -> x1, waiting for transfers between devices: 3.52 us -> 24.8 us  [exchange(): lax.all_to_all(values, axis, split_axis=0, concat_axis=0, tiled=True, axi...]
    all_to_all x2 -> x4, blocking collectives: 118 us -> 98 us  [exchange(): lax.all_to_all(values, axis, split_axis=0, concat_axis=0, tiled=True, axi...]
    all_to_all x2 -> x1, starting transfers between devices: 14.1 us -> 3.59 us  [exchange(): lax.all_to_all(values, axis, split_axis=0, concat_axis=0, tiled=True, axi...]
    pallas_call x4, Pallas kernels: 24.8 us -> 22.3 us  [the longest x1 14.2 us: whole_attention(): pl.pallas_call(whole_kernel, grid=(tokens // cell,), in_specs=[cube, row,...]
  transfers between devices with their start and end apart: 2 -> 1, of which waited for: 1 -> 1; matrix products, arithmetic and copies ran while one was open for 0% -> 0% of each run, Pallas kernels for 10% -> 3%
where the time goes in v3:
time: 150 us
  blocking collectives  98 us (65%)
  waiting for transfers between devices  24.8 us (17%)
  Pallas kernels  22.5 us (15%)
  starting transfers between devices  3.59 us (2%)
    all_to_all x4, blocking collectives, exchange(): lax.all_to_all(values, axis, split_axis=0, concat_axis=0, tiled=True, axi...  98 us
    all_to_all x1, waiting for transfers between devices, exchange(): lax.all_to_all(values, axis, split_axis=0, concat_axis=0, tiled=True, axi...  24.8 us
    pallas_call x1, Pallas kernels, whole_attention(): pl.pallas_call(whole_kernel, grid=(tokens // cell,), in_specs=[cube, row,...  14.2 us
    pallas_call x1, Pallas kernels, normalize(): pl.pallas_call(norm_kernel, grid=(steps,), in_specs=[block], out_specs=[b...  3.86 us
    all_to_all x1, starting transfers between devices, exchange(): lax.all_to_all(values, axis, split_axis=0, concat_axis=0, tiled=True, axi...  3.59 us
  transfers between devices with their start and end apart: 1, of which 1 were waited for; matrix products, arithmetic and copies ran while one was open for 0% of the time, Pallas kernels for 3%

profile of v3, /device:TPU:1, one launch (start us, length us, event | category | flops | bytes accessed | tf_op | source)
XLA Modules:
  0.0 149.9 jit_solution(13387902802742679326)
XLA Ops:
  0.0 3.9 %shard_map.37 = (bf16[8,128,512]{2,1,0:T(8,128)(2,1)}, f32[8,2,512]{2,1,0:T(2,128)S(1)}) custom-call(bf16[8,128,512]{2,1,0:T(8,128)(2,1)} %bitcast.7), custom_call_target="tpu_custom_call" | custom-call | flops 10000000 | bytes 2097152 | tf_op jit(solution)/shard_map/pallas_call | solution.py:49
  3.9 105.3 %conditional.1 = (bf16[8,128,512]{2,1,0:T(8,128)(2,1)}) conditional(s32[]{:T(128)} %convert_element_type.3, (f32[8,2,512]{2,1,0:T(2,128)S(1)}, bf16[8,128,512]{2,1,0:T(8,128)(2,1)}, bf16[512,1536]{1,0:T(8,128)(2,1)}, bf16[512,512]{1,0:T(8,128)(2,1)}) %tuple.13, (bf16[8,128,512]{2,1,0:T(8,128)(2,1)}, bf16[512,1536]{1,0:T(8,128)(2,1)}, ...), branch_computations={%region_0.1_spmd, %region_1.2_spmd} | conditional | flops 18001000448 | bytes 30605472 | solution.py:321
  3.9 22.4 %all_to_all.33.x_ref = f32[8,2,512]{2,1,0:T(2,128)S(1)} all-to-all(f32[8,2,512]{2,1,0:T(2,128)S(1)} %get-tuple-element.23), channel_id=1, replica_groups={{0,4,8,12,16,20,24,28},{32,36,40,44,48,52,56,60},{1,5,9,13,17,21,25,29}..., dimensions={0} | all-to-all | bytes 65536 | tf_op jit(solution)/shard_map/cond/branch_0_fun/all_to_all | solution.py:283
  26.3 0.2 branch_0_fun.4
  26.5 21.8 %all_to_all.34 = bf16[16,2,512]{2,1,0:T(2,128)(2,1)S(1)} all-to-all(bf16[16,2,512]{2,1,0:T(2,128)(2,1)S(1)} %get-tuple-element.24), channel_id=1, replica_groups=mesh['inline'=8,'window'=16,'replica'=4] {'window'}, dimensions={0} | all-to-all | bytes 65536 | tf_op jit(solution)/shard_map/cond/branch_0_fun/all_to_all | solution.py:283
  48.3 14.1 %all_to_all.35 = bf16[8,32,512]{2,1,0:T(8,128)(2,1)S(1)} all-to-all(bf16[8,32,512]{2,1,0:T(8,128)(2,1)S(1)} %broadcast_in_dim.7), channel_id=1, replica_groups=mesh['inline'=8,'window'=16,'replica'=4] {'inline'}, dimensions={0} | all-to-all | bytes 524288 | tf_op jit(solution)/shard_map/cond/branch_0_fun/all_to_all | solution.py:283
  62.4 3.6 %all-to-all-start.3 = ((bf16[8,128,512]{2,1,0:T(8,128)(2,1)}), bf16[8,128,512]{2,1,0:T(8,128)(2,1)S(1)}, u32[]{:S(2)}, u32[]{:S(2)}) async-start(bf16[8,128,512]{2,1,0:T(8,128)(2,1)} %get-tuple-element.25), calls=%async_computation.3 | async-start | bytes 2097152 | tf_op jit(solution)/shard_map/cond/branch_0_fun/all_to_all | solution.py:283
  66.0 0.0 copy-start
  66.0 2.9 %branch_0_fun.6 = (bf16[512,512]{1,0:T(8,128)(2,1)}, bf16[512,512]{1,0:T(8,128)(2,1)}) custom-call(bf16[512,1536]{1,0:T(8,128)(2,1)} %get-tuple-element.28.w_ref.wq_ref.wv_ref.wk_ref, bf16[512,1536]{1,0:T(8,128)(2,1)} %get-tuple-element.28.w_ref.wq_ref.wv_ref.wk_ref), custom_call_target="tpu_custom_call" | custom-call | flops 600000000 | bytes 2097152 | tf_op jit(solution)/shard_map/cond/branch_0_fun/pallas_call | solution.py:73
  68.9 0.0 copy-done
  68.9 1.4 branch_0_fun.5.glob_ref
  70.3 24.8 %all-to-all-done.3.x_ref = bf16[8,128,512]{2,1,0:T(8,128)(2,1)S(1)} async-done(((bf16[8,128,512]{2,1,0:T(8,128)(2,1)}), bf16[8,128,512]{2,1,0:T(8,128)(2,1)S(1)}, u32[]{:S(2)}, u32[]{:S(2)}) %all-to-all-start.3) | async-done | bytes 1048608 | tf_op jit(solution)/shard_map/cond/branch_0_fun/all_to_all | solution.py:283
  95.0 14.2 %branch_0_fun.7 = bf16[8,128,512]{2,1,0:T(8,128)(2,1)} custom-call(bf16[8,128,512]{2,1,0:T(8,128)(2,1)S(1)} %all-to-all-done.3.x_ref, f32[2,8,512]{2,1,0:T(8,128)S(1)} %get-tuple-element.26.own_ref.car_ref, f32[2,8,512]{2,1,0:T(8,128)S(1)} %branch_0_fun.5.glob_ref, bf16[512,1536]{1,0:T(8,128)(2,1)} %get-tuple-element.28.w_ref.wq_ref.wv_ref.wk_ref, ...), custom_call_target="tpu_custom_call" | custom-call | flops 16999999488 | bytes 6291456 | tf_op jit(solution)/shard_map/cond/branch_0_fun/pallas_call | solution.py:217
  109.2 39.7 %all_to_all.36 = bf16[8,128,512]{2,1,0:T(8,128)(2,1)S(1)} all-to-all(bf16[8,128,512]{2,1,0:T(8,128)(2,1)} %get-tuple-element.45), channel_id=1, replica_groups={{0,4,8,12,16,20,24,28},{32,36,40,44,48,52,56,60},{1,5,9,13,17,21,25,29}..., dimensions={0} | all-to-all | bytes 2097152 | tf_op jit(solution)/shard_map/all_to_all | solution.py:283
  148.9 1.0 copy.7
  (2 shorter events, 0.0 us)
Async XLA Ops:
  62.4 32.6 %all-to-all-start.3 = ((bf16[8,128,512]{2,1,0:T(8,128)(2,1)}), bf16[8,128,512]{2,1,0:T(8,128)(2,1)S(1)}, u32[]{:S(2)}, u32[]{:S(2)}) async-start(bf16[8,128,512]{2,1,0:T(8,128)(2,1)} %get-tuple-element.25), calls=%async_computation.3 | async-start | bytes 2097152 | tf_op jit(solution)/shard_map/cond/branch_0_fun/all_to_all | solution.py:283
  66.0 2.9 %copy-start = (bf16[512,1536]{1,0:T(8,128)(2,1)S(1)}, bf16[512,1536]{1,0:T(8,128)(2,1)}, u32[]{:S(2)}) copy-start(bf16[512,1536]{1,0:T(8,128)(2,1)} %get-tuple-element.28.w_ref.wq_ref.wv_ref.wk_ref) | copy-start | bytes 4718596 | tf_op jit(solution)/shard_map/cond

commit v4 on v3

--- a/solution.py
+++ b/solution.py
@@ -165,37 +165,6 @@
     return [pltpu.VMEM((count, EMBED_SPAN), BF16), half, half, half, pltpu.VMEM((HEADS, count), F32), pltpu.VMEM((EMBED_SPAN, 128), F32)]
 
 
-def local_kernel(x_ref, car_ref, wk_ref, wqt_ref, wvt_ref, out_ref, *scratch):
-    def write(rows, local):
-        out_ref[rows, :] = local
-
-    attend(x_ref, car_ref, wk_ref, wqt_ref, wvt_ref, *scratch, write)
-
-
-def local_attention(grouped, own, c, weights, wqt, wvt):
-    rows, tokens, width = grouped.shape
-    cell = WIN * WIN
-    count = rows * cell
-    whole = pl.BlockSpec((width, width), lambda i: (0, 0))
-    weights, wqt, wvt = in_hbm(weights, wqt, wvt)
-    return pl.pallas_call(
-        local_kernel,
-        grid=(1,),
-        in_specs=[
-            pl.BlockSpec((rows, cell, width), lambda i: (0, c, 0)),
-            pl.BlockSpec((1, 8, width), lambda i: (c, 0, 0)),
-            pl.BlockSpec((width, width), lambda i: (0, 1)),
-            whole,
-            whole,
-        ],
-        out_specs=pl.BlockSpec((width, count), lambda i: (0, 0)),
-        out_shape=pltpu.HBM((width, count), F32),
-        scratch_shapes=attend_scratch(),
-        compiler_params=PARAMS,
-        cost_estimate=cost(8_000_000_000, 4 << 20, 4 << 20),
-    )(grouped, own, weights, wqt, wvt)
-
-
 def whole_kernel(x_ref, car_ref, glob_ref, wk_ref, wqt_ref, wvt_ref, wo_ref, out_ref, inner_s, gl_s, *scratch):
     gl_s[...] = jnp.broadcast_to(glob_ref[0, 0:1, :], (128, EMBED_SPAN)).T
 
@@ -258,25 +227,52 @@
     )(carriers, own, weights)
 
 
-def finish_kernel(all_ref, own_ref, w_ref, wo_ref, *rest):
-    out_ref = rest[-1]
+def spread_kernel(all_ref, mine_ref, w_ref, wo_ref, out_ref):
     keys, values = carrier_match(all_ref, w_ref)
-    cell = WIN * WIN
-    for c, local_ref in enumerate(rest[:-1]):
-        glob = carrier_attention(own_ref[c, 0:1, :], w_ref, keys, values)
-        column = widen(jnp.broadcast_to(glob, (128, EMBED_SPAN)).T, local_ref.shape[1])
-        inner = (local_ref[...] + column).astype(BF16)
-        update = lax.dot_general(inner, wo_ref[...], TN, preferred_element_type=F32).astype(BF16)
-        out_ref[:, c * cell : (c + 1) * cell, :] = update.reshape(-1, cell, EMBED_SPAN)
-
-
-def finish(carriers, own, weights, w_out, local, shape):
-    return pl.pallas_call(
-        finish_kernel,
-        out_shape=jax.ShapeDtypeStruct(shape, BF16),
-        compiler_params=PARAMS,
-        cost_estimate=cost(1_000_000_000, 6 << 20, 16384),
-    )(carriers, own, weights, w_out, *in_hbm(*local))
+    cubes = mine_ref.shape[0]
+    queries = jnp.dot(mine_ref[...], w_ref[:, :EMBED_SPAN], preferred_element_type=F32)
+    queries = jnp.broadcast_to(queries[:, None, :], (cubes, HEADS, EMBED_SPAN)).reshape(cubes * HEADS, EMBED_SPAN)
+    mask = head_mask(cubes * HEADS)
+    queries = jnp.where(mask, queries, 0.0).astype(BF16)
+    s = lax.dot_general(queries, keys, NT, preferred_element_type=F32) * SCALE
+    weights = jnp.exp(s - jnp.max(s, axis=-1, keepdims=True))
+    total = jnp.sum(weights, axis=-1, keepdims=True)
+    summed = jnp.dot(weights.astype(BF16), values, preferred_element_type=F32) / total
+    glob = jnp.sum(jnp.where(mask, summed, 0.0).reshape(cubes, HEADS, EMBED_SPAN), axis=1)
+    high = glob.astype(BF16)
+    low = (glob - high.astype(F32)).astype(BF16)
+    out_ref[...] = jnp.dot(high, wo_ref[...], preferred_element_type=F32) + jnp.dot(low, wo_ref[...], preferred_element_type=F32)
+
+
+def row_glob(carriers, mine, weights, w_out):
+    return pl.pallas_call(
+        spread_kernel,
+        out_shape=jax.ShapeDtypeStruct(mine.shape, F32),
+        compiler_params=PARAMS,
+        cost_estimate=cost(800_000_000, 3 << 20, 65536),
+    )(carriers, mine, weights, w_out)
+
+
+def add_kernel(x_ref, g_ref, out_ref):
+    rows, tokens, width = x_ref.shape
+    cells = g_ref.shape[1]
+    x = x_ref[...].astype(F32).reshape(rows, cells, tokens // cells, width)
+    out_ref[...] = (x + g_ref[...][:, :, None, :]).astype(BF16).reshape(x_ref.shape)
+
+
+def add_glob(returned, glob):
+    dests, tokens, width = returned.shape
+    steps = 4
+    block = pl.BlockSpec((dests // steps, tokens, width), lambda i: (i, 0, 0))
+    return pl.pallas_call(
+        add_kernel,
+        grid=(steps,),
+        in_specs=[block, pl.BlockSpec((dests // steps,) + glob.shape[1:], lambda i: (i, 0, 0))],
+        out_specs=block,
+        out_shape=jax.ShapeDtypeStruct(returned.shape, BF16),
+        compiler_params=PARAMS,
+        cost_estimate=cost(1_000_000, 2 << 20),
+    )(returned, glob)
 
 
 def exchange(values, axis, groups=None):
@@ -288,28 +284,31 @@
 
 
 def slab_first(normed, sums, weights, w_out, groups, window):
-    width = normed.shape[-1]
+    dests, cells, width = sums.shape
     grouped = exchange(normed, "window", groups)
-    own, copies = own_carriers(grouped, sums.shape[1], window)
+    own, copies = own_carriers(grouped, cells, window)
     wqt, wvt = turn(weights)
     near = exchange(copies, "window").reshape(-1, width)
-    first = local_attention(grouped, own, 0, weights, wqt, wvt)
-    grouped, near = lax.optimization_barrier((grouped, near))
-    carriers = spread(near, "inline").reshape(-1, width)
-    second = local_attention(grouped, own, 1, weights, wqt, wvt)
-    return finish(carriers, own, weights, w_out, (first, second), grouped.shape)
+    update = whole_attention(grouped, own, jnp.zeros_like(own), weights, wqt, wvt, w_out)
+    update, near = lax.optimization_barrier((update, near))
+    returned = exchange(update, "window", groups)
+    carriers = lax.all_gather(near, "inline", axis=0, tiled=True)
+    cubes = dests * cells
+    mine = lax.dynamic_slice_in_dim(near, lax.axis_index("window") // WIN * cubes, cubes, 0)
+    return returned, row_glob(carriers, mine, weights, w_out).reshape(sums.shape)
 
 
 def carriers_first(normed, sums, weights, w_out, groups, window):
     width = normed.shape[-1]
     own, copies = own_carriers(exchange(sums, "window", groups), sums.shape[1], window)
     near = exchange(copies, "window").reshape(-1, width)
-    carriers = spread(near, "inline").reshape(-1, width)
-    normed, carriers = lax.optimization_barrier((normed, carriers))
+    normed, near = lax.optimization_barrier((normed, near))
     grouped = exchange(normed, "window", groups)
     wqt, wvt = turn(weights)
+    carriers = lax.all_gather(near, "inline", axis=0, tiled=True)
     glob = glob_of(carriers, own, weights)
-    return whole_attention(grouped, own, glob, weights, wqt, wvt, w_out)
+    update = whole_attention(grouped, own, glob, weights, wqt, wvt, w_out)
+    return exchange(update, "window", groups), jnp.zeros_like(sums)
 
 
 def body(tokens, weights, w_out):
@@ -318,13 +317,13 @@
     groups = [[h * WIN + l for l in range(WIN)] for h in range(window // WIN)]
     rows = tokens.reshape(WIN, -1, width)
     normed, sums = normalize(rows)
-    update = lax.cond(
+    returned, glob = lax.cond(
         lax.axis_index("replica") % 2 == 0,
         lambda *args: slab_first(*args, groups, window),
         lambda *args: carriers_first(*args, groups, window),
         normed, sums, weights, w_out,
     )
-    return exchange(update, "window", groups).reshape(tokens.shape)
+    return add_glob(returned, glob).reshape(tokens.shape)
 
 
 def solution(mesh):

time: 150 us -> 141 us (0.940)
  waiting for transfers between devices: 24.8 us -> 0.01 us
  blocking collectives: 98 us -> 112 us
  Pallas kernels: 22.5 us -> 25.2 us
    all_gather x0 -> x1, blocking collectives: none -> 29.4 us  [carriers_first(): carriers = lax.all_gather(near, 'inline', axis=0, tiled=True)]
    all_to_all x1, waiting for transfers between devices: 24.8 us -> 0.01 us  [exchange(): lax.all_to_all(values, axis, split_axis=0, concat_axis=0, tiled=True, axi...]
    all_to_all x4 -> x3, blocking collectives: 98 us -> 82.3 us  [exchange(): lax.all_to_all(values, axis, split_axis=0, concat_axis=0, tiled=True, axi...]
    pallas_call x0 -> x1, Pallas kernels: none -> 3.43 us  [add_glob(): pl.pallas_call(add_kernel, grid=(steps,), in_specs=[block, pl.BlockSpec((...]
  transfers between devices with their start and end apart: 1 -> 1, of which waited for: 1 -> 0; matrix products, arithmetic and copies ran while one was open for 0% -> 0% of each run, Pallas kernels for 3% -> 3%
where the time goes in v4:
time: 141 us
  blocking collectives  112 us (79%)
  Pallas kernels  25.2 us (18%)
  starting transfers between devices  3.6 us (3%)
    all_to_all x3, blocking collectives, exchange(): lax.all_to_all(values, axis, split_axis=0, concat_axis=0, tiled=True, axi...  82.3 us
    all_gather x1, blocking collectives, carriers_first(): carriers = lax.all_gather(near, 'inline', axis=0, tiled=True)  29.4 us
    pallas_call x1, Pallas kernels, whole_attention(): pl.pallas_call(whole_kernel, grid=(tokens // cell,), in_specs=[cube, row,...  13.4 us
    pallas_call x1, Pallas kernels, normalize(): pl.pallas_call(norm_kernel, grid=(steps,), in_specs=[block], out_specs=[b...  3.86 us
    all_to_all x1, starting transfers between devices, exchange(): lax.all_to_all(values, axis, split_axis=0, concat_axis=0, tiled=True, axi...  3.6 us
    pallas_call x1, Pallas kernels, add_glob(): pl.pallas_call(add_kernel, grid=(steps,), in_specs=[block, pl.BlockSpec((...  3.43 us
    pallas_call x1, Pallas kernels, turn(): pl.pallas_call(turn_kernel, grid=(1,), in_specs=[whole, pl.BlockSpec((wid...  2.87 us
  transfers between devices with their start and end apart: 1, of which 0 were waited for; matrix products, arithmetic and copies ran while one was open for 0% of the time, Pallas kernels for 3%

profile of v4, /device:TPU:1, one launch (start us, length us, event | category | flops | bytes accessed | tf_op | source)
XLA Modules:
  0.0 140.7 jit_solution(15007545369515280802)
XLA Ops:
  0.0 3.9 %shard_map.37 = (bf16[8,128,512]{2,1,0:T(8,128)(2,1)}, f32[8,2,512]{2,1,0:T(2,128)S(1)}) custom-call(bf16[8,128,512]{2,1,0:T(8,128)(2,1)} %bitcast.2), custom_call_target="tpu_custom_call" | custom-call | flops 10000000 | bytes 2097152 | tf_op jit(solution)/shard_map/pallas_call | solution.py:49
  3.9 133.4 %conditional.1 = (bf16[8,128,512]{2,1,0:T(8,128)(2,1)}, f32[8,2,512]{2,1,0:T(2,128)S(1)}) conditional(s32[]{:T(128)} %convert_element_type.3, (f32[8,2,512]{2,1,0:T(2,128)S(1)}, bf16[8,128,512]{2,1,0:T(8,128)(2,1)}, bf16[512,1536]{1,0:T(8,128)(2,1)}, bf16[512,512]{1,0:T(8,128)(2,1)}) %tuple.15, (bf16[8,128,512]{2,1,0:T(8,128)(2,1)}, ...), branch_computations={%region_0.1_spmd, %region_1.2_spmd} | conditional | flops 18400999424 | bytes 27853204 | solution.py:320
  3.9 22.4 %all_to_all.28.x_ref = f32[8,2,512]{2,1,0:T(2,128)S(1)} all-to-all(f32[8,2,512]{2,1,0:T(2,128)S(1)} %get-tuple-element.20), channel_id=1, replica_groups={{0,4,8,12,16,20,24,28},{32,36,40,44,48,52,56,60},{1,5,9,13,17,21,25,29}..., dimensions={0} | all-to-all | bytes 65536 | tf_op jit(solution)/shard_map/cond/branch_0_fun/all_to_all | solution.py:279
  26.3 0.2 branch_0_fun.4
  26.5 21.8 %all_to_all.29 = bf16[16,2,512]{2,1,0:T(2,128)(2,1)S(1)} all-to-all(bf16[16,2,512]{2,1,0:T(2,128)(2,1)S(1)} %get-tuple-element.21), channel_id=1, replica_groups=mesh['inline'=8,'window'=16,'replica'=4] {'window'}, dimensions={0} | all-to-all | bytes 65536 | tf_op jit(solution)/shard_map/cond/branch_0_fun/all_to_all | solution.py:279
  48.3 3.6 %all-to-all-start.2 = ((bf16[8,128,512]{2,1,0:T(8,128)(2,1)}), bf16[8,128,512]{2,1,0:T(8,128)(2,1)S(1)}, u32[]{:S(2)}, u32[]{:S(2)}) async-start(bf16[8,128,512]{2,1,0:T(8,128)(2,1)} %get-tuple-element.22), calls=%async_computation.2 | async-start | bytes 2097152 | tf_op jit(solution)/shard_map/cond/branch_0_fun/all_to_all | solution.py:279
  51.9 0.0 copy-start
  51.9 2.9 %branch_0_fun.6 = (bf16[512,512]{1,0:T(8,128)(2,1)}, bf16[512,512]{1,0:T(8,128)(2,1)}) custom-call(bf16[512,1536]{1,0:T(8,128)(2,1)} %get-tuple-element.25.w_ref.wq_ref.wv_ref.wk_ref, bf16[512,1536]{1,0:T(8,128)(2,1)} %get-tuple-element.25.w_ref.wq_ref.wv_ref.wk_ref), custom_call_target="tpu_custom_call" | custom-call | flops 600000000 | bytes 2097152 | tf_op jit(solution)/shard_map/cond/branch_0_fun/pallas_call | solution.py:73
  54.8 29.4 %all_gather.4.all_ref = bf16[256,512]{1,0:T(8,128)(2,1)S(1)} all-gather(bf16[32,512]{1,0:T(8,128)(2,1)S(1)} %reshape.10), channel_id=1, replica_groups=mesh['inline'=8,'window'=16,'replica'=4] {'inline'}, dimensions={0}, use_global_device_ids=true | all-gather | bytes 294912 | tf_op jit(solution)/shard_map/cond/branch_0_fun/all_gather | solution.py:308
  84.2 0.0 copy-done
  84.2 1.4 branch_0_fun.5.glob_ref
  85.5 0.0 all-to-all-done.2.x_ref
  85.6 13.4 %branch_0_fun.7 = bf16[8,128,512]{2,1,0:T(8,128)(2,1)S(1)} custom-call(bf16[8,128,512]{2,1,0:T(8,128)(2,1)S(1)} %all-to-all-done.2.x_ref, f32[2,8,512]{2,1,0:T(8,128)S(1)} %get-tuple-element.23.own_ref.car_ref, f32[2,8,512]{2,1,0:T(8,128)S(1)} %branch_0_fun.5.glob_ref, bf16[512,1536]{1,0:T(8,128)(2,1)} %get-tuple-element.25.w_ref.wq_ref.wv_ref.wk_ref, ...), custom_call_target="tpu_custom_call" | custom-call | flops 16999999488 | bytes 6291456 | tf_op jit(solution)/shard_map/cond/branch_0_fun/pallas_call | solution.py:186
  99.0 38.1 %all_to_all.30 = bf16[8,128,512]{2,1,0:T(8,128)(2,1)} all-to-all(bf16[8,128,512]{2,1,0:T(8,128)(2,1)S(1)} %branch_0_fun.7), channel_id=1, replica_groups={{0,4,8,12,16,20,24,28},{32,36,40,44,48,52,56,60},{1,5,9,13,17,21,25,29}..., dimensions={0} | all-to-all | bytes 2097152 | tf_op jit(solution)/shard_map/cond/branch_0_fun/all_to_all | solution.py:279
  137.3 3.4 %shard_map.38 = bf16[8,128,512]{2,1,0:T(8,128)(2,1)} custom-call(bf16[8,128,512]{2,1,0:T(8,128)(2,1)} %get-tuple-element.44.x_ref, f32[8,2,512]{2,1,0:T(2,128)S(1)} %get-tuple-element.45.g_ref), custom_call_target="tpu_custom_call" | custom-call | flops 1000000 | bytes 2097152 | tf_op jit(solution)/shard_map/pallas_call | solution.py:267
  (2 shorter events, 0.0 us)
Async XLA Ops:
  48.3 37.2 %all-to-all-start.2 = ((bf16[8,128,512]{2,1,0:T(8,128)(2,1)}), bf16[8,128,512]{2,1,0:T(8,128)(2,1)S(1)}, u32[]{:S(2)}, u32[]{:S(2)}) async-start(bf16[8,128,512]{2,1,0:T(8,128)(2,1)} %get-tuple-element.22), calls=%async_computation.2 | async-start | bytes 2097152 | tf_op jit(solution)/shard_map/cond/branch_0_fun/all_to_all | solution.py:279
  51.9 32.3 %copy-start = (bf16[512,1536]{1,0:T(8,128)(2,1)S(1)}, bf16[512,1536]{1,0:T(8,128)(2,1)}, u32[]{:S(2)}) copy-start(bf16[512,1536]{1,0:T(8,128)(2,1)} %get-tuple-element.25.w_ref.wq_ref.wv_ref.wk_ref) | copy-start | bytes 4718596 | tf_op jit(solution)/shard_map/cond

commit v5 on v4

--- a/solution.py
+++ b/solution.py
@@ -43,7 +43,7 @@
 
 def normalize(rows):
     dests, tokens, width = rows.shape
-    steps = 4
+    steps = 2
     cells = tokens // (WIN * WIN)
     block = pl.BlockSpec((dests // steps, tokens, width), lambda i: (i, 0, 0))
     return pl.pallas_call(
@@ -262,7 +262,7 @@
 
 def add_glob(returned, glob):
     dests, tokens, width = returned.shape
-    steps = 4
+    steps = 2
     block = pl.BlockSpec((dests // steps, tokens, width), lambda i: (i, 0, 0))
     return pl.pallas_call(
         add_kernel,
@@ -292,7 +292,7 @@
     update = whole_attention(grouped, own, jnp.zeros_like(own), weights, wqt, wvt, w_out)
     update, near = lax.optimization_barrier((update, near))
     returned = exchange(update, "window", groups)
-    carriers = lax.all_gather(near, "inline", axis=0, tiled=True)
+    carriers = gather_inline(near)
     cubes = dests * cells
     mine = lax.dynamic_slice_in_dim(near, lax.axis_index("window") // WIN * cubes, cubes, 0)
     return returned, row_glob(carriers, mine, weights, w_out).reshape(sums.shape)
@@ -305,10 +305,20 @@
     normed, near = lax.optimization_barrier((normed, near))
     grouped = exchange(normed, "window", groups)
     wqt, wvt = turn(weights)
-    carriers = lax.all_gather(near, "inline", axis=0, tiled=True)
+    carriers = gather_inline(near)
     glob = glob_of(carriers, own, weights)
     update = whole_attention(grouped, own, glob, weights, wqt, wvt, w_out)
     return exchange(update, "window", groups), jnp.zeros_like(sums)
+
+
+def gather_inline(rows):
+    count = lax.axis_size("inline")
+    step = 1
+    while step < count:
+        other = lax.ppermute(rows, "inline", [(i, i ^ step) for i in range(count)])
+        rows = jnp.concatenate([rows, other], axis=0)
+        step *= 2
+    return rows
 
 
 def body(tokens, weights, w_out):

time: 141 us -> 137 us (0.972)
  blocking collectives: 112 us -> 84.3 us
  starting transfers between devices: 3.6 us -> 16.3 us
  waiting for transfers between devices: 0.01 us -> 12.7 us
  Pallas kernels: 25.2 us -> 22.7 us
    all_gather x1 -> x0, blocking collectives: 29.4 us -> none  [carriers_first(): carriers = lax.all_gather(near, 'inline', axis=0, tiled=True)]
    ppermute x0 -> x3, starting transfers between devices: none -> 12.7 us  [gather_inline(): other = lax.ppermute(rows, 'inline', [(i, i ^ step) for i in range(count)])]
    all_to_all x1, waiting for transfers between devices: 0.01 us -> 9.12 us  [exchange(): lax.all_to_all(values, axis, split_axis=0, concat_axis=0, tiled=True, axi...]
    ppermute x0 -> x3, waiting for transfers between devices: none -> 3.6 us  [gather_inline(): other = lax.ppermute(rows, 'inline', [(i, i ^ step) for i in range(count)])]
    all_to_all x3, blocking collectives: 82.3 us -> 84.3 us  [exchange(): lax.all_to_all(values, axis, split_axis=0, concat_axis=0, tiled=True, axi...]
  transfers between devices with their start and end apart: 1 -> 4, of which waited for: 0 -> 3; matrix products, arithmetic and copies ran while one was open for 0% -> 0% of each run, Pallas kernels for 3% -> 3%
where the time goes in v5:
time: 137 us; the launch traced here: 136 us
  blocking collectives  84.3 us (62%)
  Pallas kernels  22.7 us (17%)
  starting transfers between devices  16.3 us (12%)
  waiting for transfers between devices  12.7 us (9%)
    all_to_all x3, blocking collectives, exchange(): lax.all_to_all(values, axis, split_axis=0, concat_axis=0, tiled=True, axi...  84.3 us
    pallas_call x1, Pallas kernels, whole_attention(): pl.pallas_call(whole_kernel, grid=(tokens // cell,), in_specs=[cube, row,...  13.4 us
    ppermute x3, starting transfers between devices, gather_inline(): other = lax.ppermute(rows, 'inline', [(i, i ^ step) for i in range(count)])  12.7 us
    all_to_all x1, waiting for transfers between devices, exchange(): lax.all_to_all(values, axis, split_axis=0, concat_axis=0, tiled=True, axi...  9.12 us
    all_to_all x1, starting transfers between devices, exchange(): lax.all_to_all(values, axis, split_axis=0, concat_axis=0, tiled=True, axi...  3.6 us
    ppermute x3, waiting for transfers between devices, gather_inline(): other = lax.ppermute(rows, 'inline', [(i, i ^ step) for i in range(count)])  3.6 us
    pallas_call x1, Pallas kernels, turn(): pl.pallas_call(turn_kernel, grid=(1,), in_specs=[whole, pl.BlockSpec((wid...  2.88 us
  transfers between devices with their start and end apart: 4, of which 3 were waited for; matrix products, arithmetic and copies ran while one was open for 0% of the time, Pallas kernels for 3%

profile of v5, /device:TPU:1, one launch (start us, length us, event | category | flops | bytes accessed | tf_op | source)
XLA Modules:
  0.0 136.3 jit_solution(3168594886174853319)
XLA Ops:
  0.0 2.7 %shard_map.37 = (bf16[8,128,512]{2,1,0:T(8,128)(2,1)}, f32[8,2,512]{2,1,0:T(2,128)S(1)}) custom-call(bf16[8,128,512]{2,1,0:T(8,128)(2,1)} %bitcast.2), custom_call_target="tpu_custom_call" | custom-call | flops 10000000 | bytes 2097152 | tf_op jit(solution)/shard_map/pallas_call | solution.py:49
  2.7 131.5 %conditional.1 = (bf16[8,128,512]{2,1,0:T(8,128)(2,1)}, f32[8,2,512]{2,1,0:T(2,128)S(1)}) conditional(s32[]{:T(128)} %convert_element_type.3, (f32[8,2,512]{2,1,0:T(2,128)S(1)}, bf16[8,128,512]{2,1,0:T(8,128)(2,1)}, bf16[512,1536]{1,0:T(8,128)(2,1)}, bf16[512,512]{1,0:T(8,128)(2,1)}) %tuple.15, (bf16[8,128,512]{2,1,0:T(8,128)(2,1)}, ...), branch_computations={%region_0.1_spmd, %region_1.2_spmd} | conditional | flops 18402572288 | bytes 29393412 | solution.py:330
  2.7 22.4 %all_to_all.28.x_ref = f32[8,2,512]{2,1,0:T(2,128)S(1)} all-to-all(f32[8,2,512]{2,1,0:T(2,128)S(1)} %get-tuple-element.20), channel_id=1, replica_groups={{0,4,8,12,16,20,24,28},{32,36,40,44,48,52,56,60},{1,5,9,13,17,21,25,29}..., dimensions={0} | all-to-all | bytes 65536 | tf_op jit(solution)/shard_map/cond/branch_0_fun/all_to_all | solution.py:279
  25.1 0.2 branch_0_fun.4
  25.3 21.8 %all_to_all.29 = bf16[16,2,512]{2,1,0:T(2,128)(2,1)S(1)} all-to-all(bf16[16,2,512]{2,1,0:T(2,128)(2,1)S(1)} %get-tuple-element.21), channel_id=1, replica_groups=mesh['inline'=8,'window'=16,'replica'=4] {'window'}, dimensions={0} | all-to-all | bytes 65536 | tf_op jit(solution)/shard_map/cond/branch_0_fun/all_to_all | solution.py:279
  47.1 3.6 %all-to-all-start.2 = ((bf16[8,128,512]{2,1,0:T(8,128)(2,1)}), bf16[8,128,512]{2,1,0:T(8,128)(2,1)S(1)}, u32[]{:S(2)}, u32[]{:S(2)}) async-start(bf16[8,128,512]{2,1,0:T(8,128)(2,1)} %get-tuple-element.22), calls=%async_computation.2 | async-start | bytes 2097152 | tf_op jit(solution)/shard_map/cond/branch_0_fun/all_to_all | solution.py:279
  50.7 4.6 %collective-permute-start = (bf16[32,512]{1,0:T(8,128)(2,1)S(1)}, bf16[32,512]{1,0:T(8,128)(2,1)S(1)}, u32[]{:S(2)}, u32[]{:S(2)}) collective-permute-start(bf16[32,512]{1,0:T(8,128)(2,1)S(1)} %reshape.10), channel_id=1, source_target_pairs={{0,64},{64,0},{128,192},{192,128},{256,320},{320,256},{384,448},{4... | collective-permute-start | bytes 98312 | tf_op jit(solution)/shard_map/cond/branch_0_fun/ppermute | solution.py:318
  55.4 1.5 %collective-permute-done = bf16[32,512]{1,0:T(8,128)(2,1)S(1)} collective-permute-done((bf16[32,512]{1,0:T(8,128)(2,1)S(1)}, bf16[32,512]{1,0:T(8,128)(2,1)S(1)}, u32[]{:S(2)}, u32[]{:S(2)}) %collective-permute-start) | collective-permute-done | bytes 32800 | tf_op jit(solution)/shard_map/cond/branch_0_fun/ppermute | solution.py:318
  56.9 3.2 %collective-permute-start.1 = (bf16[64,512]{1,0:T(8,128)(2,1)S(1)}, bf16[64,512]{1,0:T(8,128)(2,1)S(1)}, u32[]{:S(2)}, u32[]{:S(2)}) collective-permute-start(bf16[64,512]{1,0:T(8,128)(2,1)S(1)} %pad_maximum_fusion.2), channel_id=1, source_target_pairs={{0,128},{64,192},{128,0},{192,64},{256,384},{320,448},{384,256},{4... | collective-permute-start | bytes 196616 | tf_op jit(solution)/shard_map/cond/branch_0_fun/ppermute | solution.py:318
  60.1 2.1 %collective-permute-done.1 = bf16[64,512]{1,0:T(8,128)(2,1)S(1)} collective-permute-done((bf16[64,512]{1,0:T(8,128)(2,1)S(1)}, bf16[64,512]{1,0:T(8,128)(2,1)S(1)}, u32[]{:S(2)}, u32[]{:S(2)}) %collective-permute-start.1) | collective-permute-done | bytes 65568 | tf_op jit(solution)/shard_map/cond/branch_0_fun/ppermute | solution.py:318
  62.2 4.8 %collective-permute-start.2 = (bf16[128,512]{1,0:T(8,128)(2,1)S(1)}, bf16[128,512]{1,0:T(8,128)(2,1)S(1)}, u32[]{:S(2)}, u32[]{:S(2)}) collective-permute-start(bf16[128,512]{1,0:T(8,128)(2,1)S(1)} %pad_maximum_fusion.1), channel_id=1, source_target_pairs={{0,256},{64,320},{128,384},{192,448},{256,0},{320,64},{384,128},{4... | collective-permute-start | bytes 393224 | tf_op jit(solution)/shard_map/cond/branch_0_fun/ppermute | solution.py:318
  67.0 0.0 copy-start
  67.0 2.9 %branch_0_fun.6 = (bf16[512,512]{1,0:T(8,128)(2,1)}, bf16[512,512]{1,0:T(8,128)(2,1)}) custom-call(bf16[512,1536]{1,0:T(8,128)(2,1)} %get-tuple-element.25.w_ref.wq_ref.wv_ref.wk_ref, bf16[512,1536]{1,0:T(8,128)(2,1)} %get-tuple-element.25.w_ref.wq_ref.wv_ref.wk_ref), custom_call_target="tpu_custom_call" | custom-call | flops 600000000 | bytes 2097152 | tf_op jit(solution)/shard_map/cond/branch_0_fun/pallas_call | solution.py:73
  69.9 0.0 collective-permute-done.2
  69.9 0.0 copy-done
  69.9 1.4 %branch_0_fun.5.glob_ref = f32[2,8,512]{2,1,0:T(8,128)S(1)} custom-call(bf16[256,512]{1,0:T(8,128)(2,1)S(1)} %pad_maximum_fusion.all_ref, f32[2,8,512]{2,1,0:T(8,128)S(1)} %get-tuple-element.23.own_ref.car_ref, bf16[512,1536]{1,0:T(8,128)(2,1)S(1)} %copy-done), custom_call_target="tpu_custom_call" | custom-call | flops 400000000 | bytes 2097152 | tf_op jit(solution)/shard_map/cond/branch_0_fun/pallas_call | solution.py:222
  71.3 9.1 %all-to-all-done.2.x_ref = bf16[8,128,512]{2,1,0:T(8,128)(2,1)S(1)} async-done(((bf16[8,128,512]{2,1,0:T(8,128)(2,1)}), bf16[8,128,512]{2,1,0:T(8,128)(2,1)S(1)}, u32[]{:S(2)}, u32[]{:S(2)}) %all-to-all-start.2) | async-done | bytes 1048608 | tf_op jit(solution)/shard_map/cond/branch_0_fun/all_to_all | solution.py:279
  80.5 13.4 %branch_0_fun.7 = bf16[8,128,512]{2,1,0:T(8,128)(2,1)S(1)} custom-call(bf16[8,128,512]{2,1,0:T(8,128)(2,1)S(1)} %all-to-all-done.2.x_ref, f32[2,8,512]{2,1,0:T(8,128)S(1)} %get-tuple-element.23.own_ref.car_ref, f32[2,8,512]{2,1,0:T(8,128)S(1)} %branch_0_fun.5.glob_ref, bf16[512,1536]{1,0:T(8,128)(2,1)} %get-tuple-element.25.w_ref.wq_ref.wv_ref.wk_ref, ...), custom_call_target="tpu_custom_call" | custom-call | flops 16999999488 | bytes 6291456 | tf_op jit(solution)/shard_map/cond/branch_0_fun/pallas_call | solution.py:186
  93.9 40.1 %all_to_all.30 = bf16[8,128,512]{2,1,0:T(8,128)(2,1)} all-to-all(bf16[8,128,512]{2,1,0:T(8,128)(2,1)S(1)} %branch_0_fun.7), channel_id=1, replica_groups={{0,4,8,12,16,20,24,28},{32,36,40,44,48,52,56,60},{1,5,9,13,17,21,25,29}..., dimensions={0} | all-to-all | bytes 2097152 | tf_op jit(solution)/shard_map/cond/branch_0_fun/all_to_all | solution.py:279
  134.2 2.1 %shard_map.38 = bf16[8,128,512]{2,1,0:T(8,128)(2,1)} custom-call(bf16[8,128,512]{2,1,0:T(8,128)(2,1)} %get-tuple-element.44.x_ref, f32[8,2,512]{2,1,0:T(2,128)S(1)} %get-tuple-element.45.g_ref), custom_call_target="tpu_custom_call" | custom-call | flops 1000000 | bytes 2097152 | tf_op jit(solution)/shard_map/pallas_call | solution.py:267
  (5 shorter events, 0.1 us)
Async XLA Ops:
  47.1 33.3 %all-to-all-start.2 = ((bf16[8,128,512]{2,1,0:T(8,128)(2,1)}), bf16[8,128,512]{2,1,0:T(8,128)(2,1)S(1)}, u32[]{:S(2)}, u32[]{:S(2)}) async-start(bf16[8,128,512]{2,1,0:T(8,128)(2,1)} %get-tuple-element.22), calls=%async_computation.2 | async-start | bytes 2097152 | tf_op jit(solution)/shard_map/cond/branch_0_fun/all_to_all | solution.py:279
  50.7 6.2 %collective-permute-start = (bf16[32,512]{1,0:T(8,128)(2,1)S(1)}, bf16[32,512]{1,0:T(8,128)(2,1)S(1)}, u32[]{:S(2)}, u32[]{:S(2)}) collective-permute-start(bf16[32,512]{1,0:T(8,128)(2,1)S(1)} %reshape.10), channel_id=1, source_target_pairs={{0,64},{64,0},{128,192},{192,128},{256,320},{320,256},{384,448},{4... | collective-permute-start | bytes 98312 | tf_op jit(solution)/shard_map/cond/branch_0_fun/ppermute | solution.py:318
  56.9 5.3 %collective-permute-start.1 = (bf16[64,512]{1,0:T(8,128)(2,1)S(1)}, bf16[64,512]{1,0:T(8,128)(2,1)S(1)}, u32[]{:S(2)}, u32[]{:S(2)}) collective-permute-start(bf16[64,512]{1,0:T(8,128)(2,1)S(1)} %pad_maximum_fusion.2), channel_id=1, source_target_pairs={{0,128},{64,192},{128,0},{192,64},{256,384},{320,448},{384,256},{4... | collective-permute-start | bytes 196616 | tf_op jit(solution)/shard_map/cond/branch_0_fun/ppermute | solution.py:318
  62.2 7.7 %collective-permute-start.2 = (bf16[128,512]{1,0:T(8,128)(2,1)S(1)}, bf16[128,512]{1,0:T(8,128)(2,1)S(1)}, u32[]{:S(2)}, u32[]{:S(2)}) collective-permute-start(bf16[128,512]{1,0:T(8,128)(2,1)S(1)} %pad_maximum_fusion.1), channel_id=1, source_target_pairs={{0,256},{64,320},{128,384},{192,448},{256,0},{320,64},{384,128},{4... | collective-permute-start | bytes 393224 | tf_op jit(solution)/shard_map/cond/branch_0_fun/ppermute | solution.py:318
  67.0 2.9 %copy-start = (bf16[512,1536]{1,0:T(8,128)(2,1)S(1)}, bf16[512,1536]{1,0:T(8,128)(2,1)}, u32[]{:S(2)}) copy-start(bf16[512,1536]{1,0:T(8,128)(2,1)} %get-tuple-element.25.w_ref.wq_ref.wv_ref.wk_ref) | copy-start | bytes 4718596 | tf_op jit(solution)/shard_map/cond

commit v6 on v5

--- a/solution.py
+++ b/solution.py
@@ -67,7 +67,7 @@
 
 def turn(weights):
     width = weights.shape[0]
-    square = pltpu.HBM((width, width), BF16)
+    square = jax.ShapeDtypeStruct((width, width), BF16)
     whole = pl.BlockSpec((width, width), lambda i: (0, 0))
     (weights,) = in_hbm(weights)
     return pl.pallas_call(
@@ -148,7 +148,7 @@
         values = jnp.concatenate([vt_s[rows, :], ones], axis=0)
         o = jnp.dot(values, weights, preferred_element_type=F32)
         total = o[HEAD_DIM : HEAD_DIM + 1] + pc
-        write(rows, (o[:HEAD_DIM] + widen(vc_s[rows, :], count) * pc.astype(BF16).astype(F32)) / total)
+        write(rows, (o[:HEAD_DIM] + widen(vc_s[rows, :], count) * pc.astype(BF16).astype(F32)) * (1.0 / total))
 
     ahead = []
     for h in range(HEADS):
@@ -192,7 +192,7 @@
         scratch_shapes=[pltpu.VMEM((width, count), BF16), pltpu.VMEM((width, 128), F32)] + attend_scratch(),
         compiler_params=PARAMS,
         cost_estimate=cost(17_000_000_000, 6 << 20, 8 << 20),
-    )(grouped, own, glob, *in_hbm(weights, wqt, wvt, w_out))
+    )(grouped, own, glob, weights, wqt, wvt, w_out)
 
 
 def carrier_match(all_ref, w_ref):

time: 137 us -> 137 us (level)
  Pallas kernels: 22.7 us -> 21.3 us
  transfers between devices with their start and end apart: 4 -> 4, of which waited for: 3 -> 4; matrix products, arithmetic and copies ran while one was open for 0% -> 0% of each run, Pallas kernels for 3% -> 3%
where the time goes in v6:
time: 137 us; the launch traced here: 136 us
  blocking collectives  84.9 us (62%)
  Pallas kernels  21.3 us (16%)
  starting transfers between devices  16.3 us (12%)
  waiting for transfers between devices  13.5 us (10%)
    all_to_all x3, blocking collectives, exchange(): lax.all_to_all(values, axis, split_axis=0, concat_axis=0, tiled=True, axi...  84.9 us
    pallas_call x1, Pallas kernels, whole_attention(): pl.pallas_call(whole_kernel, grid=(tokens // cell,), in_specs=[cube, row,...  12.8 us
    ppermute x3, starting transfers between devices, gather_inline(): other = lax.ppermute(rows, 'inline', [(i, i ^ step) for i in range(count)])  12.7 us
    all_to_all x1, waiting for transfers between devices, exchange(): lax.all_to_all(values, axis, split_axis=0, concat_axis=0, tiled=True, axi...  9.34 us
    ppermute x3, waiting for transfers between devices, gather_inline(): other = lax.ppermute(rows, 'inline', [(i, i ^ step) for i in range(count)])  4.18 us
    all_to_all x1, starting transfers between devices, exchange(): lax.all_to_all(values, axis, split_axis=0, concat_axis=0, tiled=True, axi...  3.6 us
  transfers between devices with their start and end apart: 4, of which 4 were waited for; matrix products, arithmetic and copies ran while one was open for 0% of the time, Pallas kernels for 3%

profile of v6, /device:TPU:1, one launch (start us, length us, event | category | flops | bytes accessed | tf_op | source)
XLA Modules:
  0.0 136.3 jit_solution(14058586637771482093)
XLA Ops:
  0.0 2.7 %shard_map.37 = (bf16[8,128,512]{2,1,0:T(8,128)(2,1)}, f32[8,2,512]{2,1,0:T(2,128)S(1)}) custom-call(bf16[8,128,512]{2,1,0:T(8,128)(2,1)} %bitcast.2), custom_call_target="tpu_custom_call" | custom-call | flops 10000000 | bytes 2097152 | tf_op jit(solution)/shard_map/pallas_call | solution.py:49
  2.7 131.5 %conditional.1 = (bf16[8,128,512]{2,1,0:T(8,128)(2,1)}, f32[8,2,512]{2,1,0:T(2,128)S(1)}) conditional(s32[]{:T(128)} %convert_element_type.3, (f32[8,2,512]{2,1,0:T(2,128)S(1)}, bf16[8,128,512]{2,1,0:T(8,128)(2,1)}, bf16[512,1536]{1,0:T(8,128)(2,1)}, bf16[512,512]{1,0:T(8,128)(2,1)}) %tuple.15, (bf16[8,128,512]{2,1,0:T(8,128)(2,1)}, ...), branch_computations={%region_0.1_spmd, %region_1.2_spmd} | conditional | flops 18402572288 | bytes 29393412 | solution.py:330
  2.7 22.4 %all_to_all.28.x_ref = f32[8,2,512]{2,1,0:T(2,128)S(1)} all-to-all(f32[8,2,512]{2,1,0:T(2,128)S(1)} %get-tuple-element.20), channel_id=1, replica_groups={{0,4,8,12,16,20,24,28},{32,36,40,44,48,52,56,60},{1,5,9,13,17,21,25,29}..., dimensions={0} | all-to-all | bytes 65536 | tf_op jit(solution)/shard_map/cond/branch_0_fun/all_to_all | solution.py:279
  25.1 0.2 branch_0_fun.4
  25.3 21.8 %all_to_all.29 = bf16[16,2,512]{2,1,0:T(2,128)(2,1)S(1)} all-to-all(bf16[16,2,512]{2,1,0:T(2,128)(2,1)S(1)} %get-tuple-element.21), channel_id=1, replica_groups=mesh['inline'=8,'window'=16,'replica'=4] {'window'}, dimensions={0} | all-to-all | bytes 65536 | tf_op jit(solution)/shard_map/cond/branch_0_fun/all_to_all | solution.py:279
  47.1 3.6 %all-to-all-start.2 = ((bf16[8,128,512]{2,1,0:T(8,128)(2,1)}), bf16[8,128,512]{2,1,0:T(8,128)(2,1)S(1)}, u32[]{:S(2)}, u32[]{:S(2)}) async-start(bf16[8,128,512]{2,1,0:T(8,128)(2,1)} %get-tuple-element.22), calls=%async_computation.2 | async-start | bytes 2097152 | tf_op jit(solution)/shard_map/cond/branch_0_fun/all_to_all | solution.py:279
  50.7 4.6 %collective-permute-start = (bf16[32,512]{1,0:T(8,128)(2,1)S(1)}, bf16[32,512]{1,0:T(8,128)(2,1)S(1)}, u32[]{:S(2)}, u32[]{:S(2)}) collective-permute-start(bf16[32,512]{1,0:T(8,128)(2,1)S(1)} %reshape.10), channel_id=1, source_target_pairs={{0,64},{64,0},{128,192},{192,128},{256,320},{320,256},{384,448},{4... | collective-permute-start | bytes 98312 | tf_op jit(solution)/shard_map/cond/branch_0_fun/ppermute | solution.py:318
  55.4 1.5 %collective-permute-done = bf16[32,512]{1,0:T(8,128)(2,1)S(1)} collective-permute-done((bf16[32,512]{1,0:T(8,128)(2,1)S(1)}, bf16[32,512]{1,0:T(8,128)(2,1)S(1)}, u32[]{:S(2)}, u32[]{:S(2)}) %collective-permute-start) | collective-permute-done | bytes 32800 | tf_op jit(solution)/shard_map/cond/branch_0_fun/ppermute | solution.py:318
  56.9 3.2 %collective-permute-start.1 = (bf16[64,512]{1,0:T(8,128)(2,1)S(1)}, bf16[64,512]{1,0:T(8,128)(2,1)S(1)}, u32[]{:S(2)}, u32[]{:S(2)}) collective-permute-start(bf16[64,512]{1,0:T(8,128)(2,1)S(1)} %pad_maximum_fusion.2), channel_id=1, source_target_pairs={{0,128},{64,192},{128,0},{192,64},{256,384},{320,448},{384,256},{4... | collective-permute-start | bytes 196616 | tf_op jit(solution)/shard_map/cond/branch_0_fun/ppermute | solution.py:318
  60.1 2.1 %collective-permute-done.1 = bf16[64,512]{1,0:T(8,128)(2,1)S(1)} collective-permute-done((bf16[64,512]{1,0:T(8,128)(2,1)S(1)}, bf16[64,512]{1,0:T(8,128)(2,1)S(1)}, u32[]{:S(2)}, u32[]{:S(2)}) %collective-permute-start.1) | collective-permute-done | bytes 65568 | tf_op jit(solution)/shard_map/cond/branch_0_fun/ppermute | solution.py:318
  62.2 4.8 %collective-permute-start.2 = (bf16[128,512]{1,0:T(8,128)(2,1)S(1)}, bf16[128,512]{1,0:T(8,128)(2,1)S(1)}, u32[]{:S(2)}, u32[]{:S(2)}) collective-permute-start(bf16[128,512]{1,0:T(8,128)(2,1)S(1)} %pad_maximum_fusion.1), channel_id=1, source_target_pairs={{0,256},{64,320},{128,384},{192,448},{256,0},{320,64},{384,128},{4... | collective-permute-start | bytes 393224 | tf_op jit(solution)/shard_map/cond/branch_0_fun/ppermute | solution.py:318
  67.0 0.0 copy-start
  67.0 2.1 %branch_0_fun.6 = (bf16[512,512]{1,0:T(8,128)(2,1)S(1)}, bf16[512,512]{1,0:T(8,128)(2,1)S(1)}) custom-call(bf16[512,1536]{1,0:T(8,128)(2,1)} %get-tuple-element.25.w_ref.wq_ref.wv_ref.wk_ref, bf16[512,1536]{1,0:T(8,128)(2,1)} %get-tuple-element.25.w_ref.wq_ref.wv_ref.wk_ref), custom_call_target="tpu_custom_call" | custom-call | flops 600000000 | bytes 2097152 | tf_op jit(solution)/shard_map/cond/branch_0_fun/pallas_call | solution.py:73
  69.1 0.0 copy-start.2
  69.1 0.6 collective-permute-done.2
  69.7 0.0 copy-done
  69.7 1.4 %branch_0_fun.5.glob_ref = f32[2,8,512]{2,1,0:T(8,128)S(1)} custom-call(bf16[256,512]{1,0:T(8,128)(2,1)S(1)} %pad_maximum_fusion.all_ref, f32[2,8,512]{2,1,0:T(8,128)S(1)} %get-tuple-element.23.own_ref.car_ref, bf16[512,1536]{1,0:T(8,128)(2,1)S(1)} %copy-done), custom_call_target="tpu_custom_call" | custom-call | flops 400000000 | bytes 2097152 | tf_op jit(solution)/shard_map/cond/branch_0_fun/pallas_call | solution.py:222
  71.1 9.3 %all-to-all-done.2.x_ref = bf16[8,128,512]{2,1,0:T(8,128)(2,1)S(1)} async-done(((bf16[8,128,512]{2,1,0:T(8,128)(2,1)}), bf16[8,128,512]{2,1,0:T(8,128)(2,1)S(1)}, u32[]{:S(2)}, u32[]{:S(2)}) %all-to-all-start.2) | async-done | bytes 1048608 | tf_op jit(solution)/shard_map/cond/branch_0_fun/all_to_all | solution.py:279
  80.5 0.0 copy-done.2
  80.5 12.8 %branch_0_fun.7 = bf16[8,128,512]{2,1,0:T(8,128)(2,1)S(1)} custom-call(bf16[8,128,512]{2,1,0:T(8,128)(2,1)S(1)} %all-to-all-done.2.x_ref, f32[2,8,512]{2,1,0:T(8,128)S(1)} %get-tuple-element.23.own_ref.car_ref, f32[2,8,512]{2,1,0:T(8,128)S(1)} %branch_0_fun.5.glob_ref, bf16[512,1536]{1,0:T(8,128)(2,1)} %get-tuple-element.25.w_ref.wq_ref.wv_ref.wk_ref, ...), custom_call_target="tpu_custom_call" | custom-call | flops 16999999488 | bytes 6291456 | tf_op jit(solution)/shard_map/cond/branch_0_fun/pallas_call | solution.py:186
  93.3 40.7 %all_to_all.30 = bf16[8,128,512]{2,1,0:T(8,128)(2,1)} all-to-all(bf16[8,128,512]{2,1,0:T(8,128)(2,1)S(1)} %branch_0_fun.7), channel_id=1, replica_groups={{0,4,8,12,16,20,24,28},{32,36,40,44,48,52,56,60},{1,5,9,13,17,21,25,29}..., dimensions={0} | all-to-all | bytes 2097152 | tf_op jit(solution)/shard_map/cond/branch_0_fun/all_to_all | solution.py:279
  134.2 2.1 %shard_map.38 = bf16[8,128,512]{2,1,0:T(8,128)(2,1)} custom-call(bf16[8,128,512]{2,1,0:T(8,128)(2,1)} %get-tuple-element.44.x_ref, f32[8,2,512]{2,1,0:T(2,128)S(1)} %get-tuple-element.45.g_ref), custom_call_target="tpu_custom_call" | custom-call | flops 1000000 | bytes 2097152 | tf_op jit(solution)/shard_map/pallas_call | solution.py:267
  (5 shorter events, 0.1 us)
Async XLA Ops:
  47.1 33.3 %all-to-all-start.2 = ((bf16[8,128,512]{2,1,0:T(8,128)(2,1)}), bf16[8,128,512]{2,1,0:T(8,128)(2,1)S(1)}, u32[]{:S(2)}, u32[]{:S(2)}) async-start(bf16[8,128,512]{2,1,0:T(8,128)(2,1)} %get-tuple-element.22), calls=%async_computation.2 | async-start | bytes 2097152 | tf_op jit(solution)/shard_map/cond/branch_0_fun/all_to_all | solution.py:279
  50.7 6.2 %collective-permute-start = (bf16[32,512]{1,0:T(8,128)(2,1)S(1)}, bf16[32,512]{1,0:T(8,128)(2,1)S(1)}, u32[]{:S(2)}, u32[]{:S(2)}) collective-permute-start(bf16[32,512]{1,0:T(8,128)(2,1)S(1)} %reshape.10), channel_id=1, source_target_pairs={{0,64},{64,0},{128,192},{192,128},{256,320},{320,256},{384,448},{4... | collective-permute-start | bytes 98312 | tf_op jit(solution)/shard_map/cond/branch_0_fun/ppermute | solution.py:318
  56.9 5.3 %collective-permute-start.1 = (bf16[64,512]{1,0:T(8,128)(2,1)S(1)}, bf16[64,512]{1,0:T(8,128)(2,1)S(1)}, u32[]{:S(2)}, u32[]{:S(2)}) collective-permute-start(bf16[64,512]{1,0:T(8,128)(2,1)S(1)} %pad_maximum_fusion.2), channel_id=1, source_target_pairs={{0,128},{64,192},{128,0},{192,64},{256,384},{320,448},{384,256},{4... | collective-permute-start | bytes 196616 | tf_op jit(solution)/shard_map/cond/branch_0_fun/ppermute | solution.py:318
  62.2 7.5 %collective-permute-start.2 = (bf16[128,512]{1,0:T(8,128)(2,1)S(1)}, bf16[128,512]{1,0:T(8,128)(2,1)S(1)}, u32[]{:S(2)}, u32[]{:S(2)}) collective-permute-start(bf16[128,512]{1,0:T(8,128)(2,1)S(1)} %pad_maximum_fusion.1), channel_id=1, source_target_pairs={{0,256},{64,320},{128,384},{192,448},{256,0},{320,64},{384,128},{4... | collective-permute-start | bytes 393224 | tf_op jit(solution)/shard_map/cond/branch_0_fun/ppermute | solution.py:318
  67.0 2.7 %copy-start = (bf16[512,1536]{1,0:T(8,128)(2,1)S(1)}, bf16[512,1536]{1,0:T(8,128)(2,1)}, u32[]{:S(2)}) copy-start(bf16[512,1536]{1,0:T(8,128)(2,1)} %get-tuple-element.25.w_ref.wq_ref.wv_ref.wk_ref) | copy-start | bytes 4718596 | tf_op jit(solution)/shard_map/cond
  69.1 11.4 %copy-start.2 = (bf16[512,512]{1,0:T(8,128)(2,1)S(1)}, bf16[512,512]{1,0:T(8,128)(2,1)}, u32[]{:S(2)}) copy-start(bf16[512,512]{1,0:T(8,128)(2,1)} %get-tuple-element.28.wo_ref) | copy-start | bytes 1572868 | tf_op jit(solution)/shard_map/cond

commit v7 on v6

--- a/solution.py
+++ b/solution.py
@@ -299,16 +299,20 @@
 
 
 def carriers_first(normed, sums, weights, w_out, groups, window):
-    width = normed.shape[-1]
-    own, copies = own_carriers(exchange(sums, "window", groups), sums.shape[1], window)
-    near = exchange(copies, "window").reshape(-1, width)
-    normed, near = lax.optimization_barrier((normed, near))
+    dests, cells, width = sums.shape
+    own, copies = own_carriers(exchange(sums, "window", groups), cells, window)
+    normed, copies = lax.optimization_barrier((normed, copies))
     grouped = exchange(normed, "window", groups)
     wqt, wvt = turn(weights)
+    grouped, copies = lax.optimization_barrier((grouped, copies))
+    near = exchange(copies, "window").reshape(-1, width)
+    update = whole_attention(grouped, own, jnp.zeros_like(own), weights, wqt, wvt, w_out)
+    update, near = lax.optimization_barrier((update, near))
+    returned = exchange(update, "window", groups)
     carriers = gather_inline(near)
-    glob = glob_of(carriers, own, weights)
-    update = whole_attention(grouped, own, glob, weights, wqt, wvt, w_out)
-    return exchange(update, "window", groups), jnp.zeros_like(sums)
+    cubes = dests * cells
+    mine = lax.dynamic_slice_in_dim(near, lax.axis_index("window") // WIN * cubes, cubes, 0)
+    return returned, row_glob(carriers, mine, weights, w_out).reshape(sums.shape)
 
 
 def gather_inline(rows):

time: 137 us -> 150 us (1.095)
  blocking collectives: 84.9 us -> 22.4 us
  waiting for transfers between devices: 13.5 us -> 71.6 us
  starting transfers between devices: 16.3 us -> 33 us
    all_to_all x3 -> x1, blocking collectives: 84.9 us -> 22.4 us  [exchange(): lax.all_to_all(values, axis, split_axis=0, concat_axis=0, tiled=True, axi...]
    all_to_all x1 -> x3, waiting for transfers between devices: 9.34 us -> 64.7 us  [exchange(): lax.all_to_all(values, axis, split_axis=0, concat_axis=0, tiled=True, axi...]
    all_to_all x1 -> x3, starting transfers between devices: 3.6 us -> 20.4 us  [exchange(): lax.all_to_all(values, axis, split_axis=0, concat_axis=0, tiled=True, axi...]
    ppermute x3, waiting for transfers between devices: 4.18 us -> 6.87 us  [gather_inline(): other = lax.ppermute(rows, 'inline', [(i, i ^ step) for i in range(count)])]
  transfers between devices with their start and end apart: 4 -> 6, of which waited for: 4 -> 5; matrix products, arithmetic and copies ran while one was open for 0% -> 0% of each run, Pallas kernels for 3% -> 11%
where the time goes in v7:
time: 150 us
  waiting for transfers between devices  71.6 us (48%)
  starting transfers between devices  33 us (22%)
  Pallas kernels  22.5 us (15%)
  blocking collectives  22.4 us (15%)
    all_to_all x3, waiting for transfers between devices, exchange(): lax.all_to_all(values, axis, split_axis=0, concat_axis=0, tiled=True, axi...  64.7 us
    all_to_all x1, blocking collectives, exchange(): lax.all_to_all(values, axis, split_axis=0, concat_axis=0, tiled=True, axi...  22.4 us
    all_to_all x3, starting transfers between devices, exchange(): lax.all_to_all(values, axis, split_axis=0, concat_axis=0, tiled=True, axi...  20.4 us
    pallas_call x1, Pallas kernels, whole_attention(): pl.pallas_call(whole_kernel, grid=(tokens // cell,), in_specs=[cube, row,...  13.7 us
    ppermute x3, starting transfers between devices, gather_inline(): other = lax.ppermute(rows, 'inline', [(i, i ^ step) for i in range(count)])  12.6 us
    ppermute x3, waiting for transfers between devices, gather_inline(): other = lax.ppermute(rows, 'inline', [(i, i ^ step) for i in range(count)])  6.87 us
  transfers between devices with their start and end apart: 6, of which 5 were waited for; matrix products, arithmetic and copies ran while one was open for 0% of the time, Pallas kernels for 11%

profile of v7, /device:TPU:1, one launch (start us, length us, event | category | flops | bytes accessed | tf_op | source)
XLA Modules:
  0.0 149.7 jit_solution(258652600444864051)
XLA Ops:
  0.0 2.7 %shard_map.37 = (bf16[8,128,512]{2,1,0:T(8,128)(2,1)}, f32[8,2,512]{2,1,0:T(2,128)S(1)}) custom-call(bf16[8,128,512]{2,1,0:T(8,128)(2,1)} %bitcast.2), custom_call_target="tpu_custom_call" | custom-call | flops 10000000 | bytes 2097152 | tf_op jit(solution)/shard_map/pallas_call | solution.py:49
  2.7 144.9 %conditional.1 = (bf16[8,128,512]{2,1,0:T(8,128)(2,1)}, f32[8,2,512]{2,1,0:T(2,128)S(1)}) conditional(s32[]{:T(128)} %convert_element_type.3, (f32[8,2,512]{2,1,0:T(2,128)S(1)}, bf16[8,128,512]{2,1,0:T(8,128)(2,1)}, bf16[512,1536]{1,0:T(8,128)(2,1)}, bf16[512,512]{1,0:T(8,128)(2,1)}) %tuple.17, (bf16[8,128,512]{2,1,0:T(8,128)(2,1)}, ...), branch_computations={%region_0.1_spmd, %region_1.2_spmd} | conditional | flops 18402572288 | bytes 29458948 | solution.py:334
  2.7 22.4 %all_to_all.28.x_ref = f32[8,2,512]{2,1,0:T(2,128)S(1)} all-to-all(f32[8,2,512]{2,1,0:T(2,128)S(1)} %get-tuple-element.20), channel_id=1, replica_groups={{0,4,8,12,16,20,24,28},{32,36,40,44,48,52,56,60},{1,5,9,13,17,21,25,29}..., dimensions={0} | all-to-all | bytes 65536 | tf_op jit(solution)/shard_map/cond/branch_0_fun/all_to_all | solution.py:279
  25.1 0.8 branch_0_fun.4
  25.9 3.6 %all-to-all-start.1 = ((bf16[8,128,512]{2,1,0:T(8,128)(2,1)}), bf16[8,128,512]{2,1,0:T(8,128)(2,1)S(1)}, u32[]{:S(2)}, u32[]{:S(2)}) async-start(bf16[8,128,512]{2,1,0:T(8,128)(2,1)} %get-tuple-element.22), calls=%async_computation.1 | async-start | bytes 2097152 | tf_op jit(solution)/shard_map/cond/branch_0_fun/all_to_all | solution.py:279
  29.5 0.0 copy-start.2
  29.5 2.0 %branch_0_fun.5 = (bf16[512,512]{1,0:T(8,128)(2,1)S(1)}, bf16[512,512]{1,0:T(8,128)(2,1)S(1)}) custom-call(bf16[512,1536]{1,0:T(8,128)(2,1)} %get-tuple-element.26.wq_ref.wv_ref.wk_ref.w_ref, bf16[512,1536]{1,0:T(8,128)(2,1)} %get-tuple-element.26.wq_ref.wv_ref.wk_ref.w_ref), custom_call_target="tpu_custom_call" | custom-call | flops 600000000 | bytes 2097152 | tf_op jit(solution)/shard_map/cond/branch_0_fun/pallas_call | solution.py:73
  31.5 37.5 %all-to-all-done.1.x_ref = bf16[8,128,512]{2,1,0:T(8,128)(2,1)S(1)} async-done(((bf16[8,128,512]{2,1,0:T(8,128)(2,1)}), bf16[8,128,512]{2,1,0:T(8,128)(2,1)S(1)}, u32[]{:S(2)}, u32[]{:S(2)}) %all-to-all-start.1) | async-done | bytes 1048608 | tf_op jit(solution)/shard_map/cond/branch_0_fun/all_to_all | solution.py:279
  69.0 7.4 %all-to-all-start.2 = ((bf16[16,2,512]{2,1,0:T(2,128)(2,1)}), bf16[16,2,512]{2,1,0:T(2,128)(2,1)S(1)}, u32[]{:S(2)}, u32[]{:S(2)}) async-start(bf16[16,2,512]{2,1,0:T(2,128)(2,1)} %get-tuple-element.30), calls=%async_computation.2 | async-start | bytes 65536 | tf_op jit(solution)/shard_map/cond/branch_0_fun/all_to_all | solution.py:279
  76.4 0.0 copy-done.2
  76.4 13.7 %branch_0_fun.6 = bf16[8,128,512]{2,1,0:T(8,128)(2,1)} custom-call(bf16[8,128,512]{2,1,0:T(8,128)(2,1)S(1)} %all-to-all-done.1.x_ref, f32[2,8,512]{2,1,0:T(8,128)S(1)} %get-tuple-element.25.car_ref, f32[2,8,512]{2,1,0:T(8,128)S(1)} %broadcast_1_glob_ref.0.glob_ref, bf16[512,1536]{1,0:T(8,128)(2,1)} %get-tuple-element.26.wq_ref.wv_ref.wk_ref.w_ref, ...), custom_call_target="tpu_custom_call" | custom-call | flops 16999999488 | bytes 6291456 | tf_op jit(solution)/shard_map/cond/branch_0_fun/pallas_call | solution.py:186
  90.1 0.0 copy-start
  90.1 0.0 all-to-all-done.2
  90.1 9.4 %all-to-all-start.3 = ((bf16[8,128,512]{2,1,0:T(8,128)(2,1)}), bf16[8,128,512]{2,1,0:T(8,128)(2,1)}, u32[]{:S(2)}, u32[]{:S(2)}) async-start(bf16[8,128,512]{2,1,0:T(8,128)(2,1)} %branch_0_fun.6), calls=%async_computation.3 | async-start | bytes 2097152 | tf_op jit(solution)/shard_map/cond/branch_0_fun/all_to_all | solution.py:279
  99.5 4.6 %collective-permute-start = (bf16[32,512]{1,0:T(8,128)(2,1)S(1)}, bf16[32,512]{1,0:T(8,128)(2,1)S(1)}, u32[]{:S(2)}, u32[]{:S(2)}) collective-permute-start(bf16[32,512]{1,0:T(8,128)(2,1)S(1)} %reshape.12), channel_id=1, source_target_pairs={{0,64},{64,0},{128,192},{192,128},{256,320},{320,256},{384,448},{4... | collective-permute-start | bytes 98312 | tf_op jit(solution)/shard_map/cond/branch_0_fun/ppermute | solution.py:322
  104.2 1.9 %collective-permute-done = bf16[32,512]{1,0:T(8,128)(2,1)S(1)} collective-permute-done((bf16[32,512]{1,0:T(8,128)(2,1)S(1)}, bf16[32,512]{1,0:T(8,128)(2,1)S(1)}, u32[]{:S(2)}, u32[]{:S(2)}) %collective-permute-start) | collective-permute-done | bytes 32800 | tf_op jit(solution)/shard_map/cond/branch_0_fun/ppermute | solution.py:322
  106.1 3.2 %collective-permute-start.1 = (bf16[64,512]{1,0:T(8,128)(2,1)S(1)}, bf16[64,512]{1,0:T(8,128)(2,1)S(1)}, u32[]{:S(2)}, u32[]{:S(2)}) collective-permute-start(bf16[64,512]{1,0:T(8,128)(2,1)S(1)} %pad_maximum_fusion.2), channel_id=1, source_target_pairs={{0,128},{64,192},{128,0},{192,64},{256,384},{320,448},{384,256},{4... | collective-permute-start | bytes 196616 | tf_op jit(solution)/shard_map/cond/branch_0_fun/ppermute | solution.py:322
  109.3 2.2 %collective-permute-done.1 = bf16[64,512]{1,0:T(8,128)(2,1)S(1)} collective-permute-done((bf16[64,512]{1,0:T(8,128)(2,1)S(1)}, bf16[64,512]{1,0:T(8,128)(2,1)S(1)}, u32[]{:S(2)}, u32[]{:S(2)}) %collective-permute-start.1) | collective-permute-done | bytes 65568 | tf_op jit(solution)/shard_map/cond/branch_0_fun/ppermute | solution.py:322
  111.5 4.8 %collective-permute-start.2 = (bf16[128,512]{1,0:T(8,128)(2,1)S(1)}, bf16[128,512]{1,0:T(8,128)(2,1)S(1)}, u32[]{:S(2)}, u32[]{:S(2)}) collective-permute-start(bf16[128,512]{1,0:T(8,128)(2,1)S(1)} %pad_maximum_fusion.1), channel_id=1, source_target_pairs={{0,256},{64,320},{128,384},{192,448},{256,0},{320,64},{384,128},{4... | collective-permute-start | bytes 393224 | tf_op jit(solution)/shard_map/cond/branch_0_fun/ppermute | solution.py:322
  116.4 2.8 %collective-permute-done.2 = bf16[128,512]{1,0:T(8,128)(2,1)S(1)} collective-permute-done((bf16[128,512]{1,0:T(8,128)(2,1)S(1)}, bf16[128,512]{1,0:T(8,128)(2,1)S(1)}, u32[]{:S(2)}, u32[]{:S(2)}) %collective-permute-start.2) | collective-permute-done | bytes 131104 | tf_op jit(solution)/shard_map/cond/branch_0_fun/ppermute | solution.py:322
  119.1 0.0 copy-done
  119.1 1.2 branch_0_fun.7
  120.4 27.2 %all-to-all-done.3 = bf16[8,128,512]{2,1,0:T(8,128)(2,1)} async-done(((bf16[8,128,512]{2,1,0:T(8,128)(2,1)}), bf16[8,128,512]{2,1,0:T(8,128)(2,1)}, u32[]{:S(2)}, u32[]{:S(2)}) %all-to-all-start.3) | async-done | bytes 1048608 | tf_op jit(solution)/shard_map/cond/branch_0_fun/all_to_all | solution.py:279
  147.6 2.1 %shard_map.38 = bf16[8,128,512]{2,1,0:T(8,128)(2,1)} custom-call(bf16[8,128,512]{2,1,0:T(8,128)(2,1)} %get-tuple-element.48.x_ref, f32[8,2,512]{2,1,0:T(2,128)S(1)} %get-tuple-element.49.g_ref), custom_call_target="tpu_custom_call" | custom-call | flops 1000000 | bytes 2097152 | tf_op jit(solution)/shard_map/pallas_call | solution.py:267
  (7 shorter events, 0.1 us)
Async XLA Ops:
  25.9 43.1 %all-to-all-start.1 = ((bf16[8,128,512]{2,1,0:T(8,128)(2,1)}), bf16[8,128,512]{2,1,0:T(8,128)(2,1)S(1)}, u32[]{:S(2)}, u32[]{:S(2)}) async-start(bf16[8,128,512]{2,1,0:T(8,128)(2,1)} %get-tuple-element.22), calls=%async_computation.1 | async-start | bytes 2097152 | tf_op jit(solution)/shard_map/cond/branch_0_fun/all_to_all | solution.py:279
  29.5 47.0 %copy-start.2 = (bf16[512,512]{1,0:T(8,128)(2,1)S(1)}, bf16[512,512]{1,0:T(8,128)(2,1)}, u32[]{:S(2)}) copy-start(bf16[512,512]{1,0:T(8,128)(2,1)} %get-tuple-element.29.wo_ref) | copy-start | bytes 1572868 | tf_op jit(solution)/shard_map/cond
  69.0 21.1 %all-to-all-start.2 = ((bf16[16,2,512]{2,1,0:T(2,128)(2,1)}), bf16[16,2,512]{2,1,0:T(2,128)(2,1)S(1)}, u32[]{:S(2)}, u32[]{:S(2)}) async-start(bf16[16,2,512]{2,1,0:T(2,128)(2,1)} %get-tuple-element.30), calls=%async_computation.2 | async-start | bytes 65536 | tf_op jit(solution)/shard_map/cond/branch_0_fun/all_to_all | solution.py:279
  90.1 29.0 %copy-start = (bf16[512,1536]{1,0:T(8,128)(2,1)S(1)}, bf16[512,1536]{1,0:T(8,128)(2,1)}, u32[]{:S(2)}) copy-start(bf16[512,1536]{1,0:T(8,128)(2,1)} %get-tuple-element.26.wq_ref.wv_ref.wk_ref.w_ref) | copy-start | bytes 4718596 | tf_op jit(solution)/shard_map/cond
  90.1 57.4 %all-to-all-start.3 = ((bf16[8,128,512]{2,1,0:T(8,128)(2,1)}), bf16[8,128,512]{2,1,0:T(8,128)(2,1)}, u32[]{:S(2)}, u32[]{:S(2)}) async-start(bf16[8,128,512]{2,1,0:T(8,128)(2,1)} %branch_0_fun.6), calls=%async_computation.3 | async-start | bytes 2097152 | tf_op jit(solution)/shard_map/cond/branch_0_fun/all_to_all | solution.py:279
  99.5 6.6 %collective-permute-start = (bf16[32,512]{1,0:T(8,128)(2,1)S(1)}, bf16[32,512]{1,0:T(8,128)(2,1)S(1)}, u32[]{:S(2)}, u32[]{:S(2)}) collective-permute-start(bf16[32,512]{1,0:T(8,128)(2,1)S(1)} %reshape.12), channel_id=1, source_target_pairs={{0,64},{64,0},{128,192},{192,128},{256,320},{320,256},{384,448},{4... | collective-permute-start | bytes 98312 | tf_op jit(solution)/shard_map/cond/branch_0_fun/ppermute | solution.py:322
  106.1 5.4 %collective-permute-start.1 = (bf16[64,512]{1,0:T(8,128)(2,1)S(1)}, bf16[64,512]{1,0:T(8,128)(2,1)S(1)}, u32[]{:S(2)}, u32[]{:S(2)}) collective-permute-start(bf16[64,512]{1,0:T(8,128)(2,1)S(1)} %pad_maximum_fusion.2), channel_id=1, source_target_pairs={{0,128},{64,192},{128,0},{192,64},{256,384},{320,448},{384,256},{4... | collective-permute-start | bytes 196616 | tf_op jit(solution)/shard_map/cond/branch_0_fun/ppermute | solution.py:322
  111.5 7.6 %collective-permute-start.2 = (bf16[128,512]{1,0:T(8,128)(2,1)S(1)}, bf16[128,512]{1,0:T(8,128)(2,1)S(1)}, u32[]{:S(2)}, u32[]{:S(2)}) collective-permute-start(bf16[128,512]{1,0:T(8,128)(2,1)S(1)} %pad_maximum_fusion.1), channel_id=1, source_target_pairs={{0,256},{64,320},{128,384},{192,448},{256,0},{320,64},{384,128},{4... | collective-permute-start | bytes 393224 | tf_op jit(solution)/shard_map/cond/branch_0_fun/ppermute | solution.py:322

commit v8 on v6

--- a/solution.py
+++ b/solution.py
@@ -33,6 +33,10 @@
     return center * lax.rsqrt(spread + EPSILON)
 
 
+def plain_norm_kernel(x_ref, normed_ref):
+    normed_ref[...] = standardize(x_ref[...].astype(F32)).astype(BF16)
+
+
 def norm_kernel(x_ref, normed_ref, sums_ref):
     dests, tokens, width = x_ref.shape
     cell = WIN * WIN
@@ -41,17 +45,19 @@
     sums_ref[...] = jnp.sum(normed.astype(F32).reshape(dests, tokens // cell, cell, width), axis=2)
 
 
-def normalize(rows):
+def normalize(rows, with_sums):
     dests, tokens, width = rows.shape
     steps = 2
     cells = tokens // (WIN * WIN)
     block = pl.BlockSpec((dests // steps, tokens, width), lambda i: (i, 0, 0))
-    return pl.pallas_call(
-        norm_kernel,
+    sums_block = pl.BlockSpec((dests // steps, cells, width), lambda i: (i, 0, 0))
+    sums_shape = jax.ShapeDtypeStruct((dests, cells, width), F32)
+    return pl.pallas_call(
+        norm_kernel if with_sums else plain_norm_kernel,
         grid=(steps,),
         in_specs=[block],
-        out_specs=[block, pl.BlockSpec((dests // steps, cells, width), lambda i: (i, 0, 0))],
-        out_shape=[jax.ShapeDtypeStruct(rows.shape, BF16), jax.ShapeDtypeStruct((dests, cells, width), F32)],
+        out_specs=[block, sums_block] if with_sums else [block],
+        out_shape=[jax.ShapeDtypeStruct(rows.shape, BF16)] + ([sums_shape] if with_sums else []),
         compiler_params=PARAMS,
         cost_estimate=cost(10_000_000, 2 << 20),
     )(*in_hbm(rows))
@@ -283,8 +289,10 @@
     return exchange(jnp.broadcast_to(values[None], (lax.axis_size(axis),) + values.shape), axis)
 
 
-def slab_first(normed, sums, weights, w_out, groups, window):
-    dests, cells, width = sums.shape
+def slab_first(rows, weights, w_out, groups, window):
+    dests, tokens, width = rows.shape
+    cells = tokens // (WIN * WIN)
+    (normed,) = normalize(rows, False)
     grouped = exchange(normed, "window", groups)
     own, copies = own_carriers(grouped, cells, window)
     wqt, wvt = turn(weights)
@@ -295,10 +303,11 @@
     carriers = gather_inline(near)
     cubes = dests * cells
     mine = lax.dynamic_slice_in_dim(near, lax.axis_index("window") // WIN * cubes, cubes, 0)
-    return returned, row_glob(carriers, mine, weights, w_out).reshape(sums.shape)
-
-
-def carriers_first(normed, sums, weights, w_out, groups, window):
+    return returned, row_glob(carriers, mine, weights, w_out).reshape(dests, cells, width)
+
+
+def carriers_first(rows, weights, w_out, groups, window):
+    normed, sums = normalize(rows, True)
     width = normed.shape[-1]
     own, copies = own_carriers(exchange(sums, "window", groups), sums.shape[1], window)
     near = exchange(copies, "window").reshape(-1, width)
@@ -326,12 +335,11 @@
     width = tokens.shape[-1]
     groups = [[h * WIN + l for l in range(WIN)] for h in range(window // WIN)]
     rows = tokens.reshape(WIN, -1, width)
-    normed, sums = normalize(rows)
     returned, glob = lax.cond(
         lax.axis_index("replica") % 2 == 0,
         lambda *args: slab_first(*args, groups, window),
         lambda *args: carriers_first(*args, groups, window),
-        normed, sums, weights, w_out,
+        rows, weights, w_out,
     )
     return add_glob(returned, glob).reshape(tokens.shape)
 

time: 137 us -> 137 us (level)
  no operation moved by 1% of the time
where the time goes in v8:
time: 137 us; the launch traced here: 136 us
  blocking collectives  84.6 us (62%)
  Pallas kernels  21.3 us (16%)
  starting transfers between devices  16.3 us (12%)
  waiting for transfers between devices  13.5 us (10%)
    all_to_all x3, blocking collectives, exchange(): lax.all_to_all(values, axis, split_axis=0, concat_axis=0, tiled=True, axi...  84.6 us
    pallas_call x1, Pallas kernels, whole_attention(): pl.pallas_call(whole_kernel, grid=(tokens // cell,), in_specs=[cube, row,...  12.9 us
    ppermute x3, starting transfers between devices, gather_inline(): other = lax.ppermute(rows, 'inline', [(i, i ^ step) for i in range(count)])  12.7 us
    all_to_all x1, waiting for transfers between devices, exchange(): lax.all_to_all(values, axis, split_axis=0, concat_axis=0, tiled=True, axi...  9.34 us
    ppermute x3, waiting for transfers between devices, gather_inline(): other = lax.ppermute(rows, 'inline', [(i, i ^ step) for i in range(count)])  4.19 us
    all_to_all x1, starting transfers between devices, exchange(): lax.all_to_all(values, axis, split_axis=0, concat_axis=0, tiled=True, axi...  3.63 us
  transfers between devices with their start and end apart: 4, of which 4 were waited for; matrix products, arithmetic and copies ran while one was open for 0% of the time, Pallas kernels for 3%

profile of v8, /device:TPU:1, one launch (start us, length us, event | category | flops | bytes accessed | tf_op | source)
XLA Modules:
  0.0 136.1 jit_solution(3952329410907220795)
XLA Ops:
  0.0 134.0 %conditional.1 = (bf16[8,128,512]{2,1,0:T(8,128)(2,1)}, f32[8,2,512]{2,1,0:T(2,128)S(1)}) conditional(s32[]{:T(128)} %convert_element_type.3, (bf16[8,128,512]{2,1,0:T(8,128)(2,1)}, bf16[512,1536]{1,0:T(8,128)(2,1)}, bf16[512,512]{1,0:T(8,128)(2,1)}) %tuple.18, (bf16[8,128,512]{2,1,0:T(8,128)(2,1)}, bf16[512,1536]{1,0:T(8,128)(2,1)}, ...), branch_computations={%region_0.1_spmd, %region_1.2_spmd} | conditional | flops 18412572672 | bytes 31490564 | solution.py:338
  0.0 2.7 %branch_0_fun.5 = (bf16[8,128,512]{2,1,0:T(8,128)(2,1)}, f32[8,2,512]{2,1,0:T(2,128)S(1)}) custom-call(bf16[8,128,512]{2,1,0:T(8,128)(2,1)} %get-tuple-element.17.x_ref), custom_call_target="tpu_custom_call" | custom-call | flops 10000000 | bytes 2097152 | tf_op jit(solution)/shard_map/cond/branch_0_fun/pallas_call | solution.py:55
  2.7 22.4 %all_to_all.28.x_ref = f32[8,2,512]{2,1,0:T(2,128)S(1)} all-to-all(f32[8,2,512]{2,1,0:T(2,128)S(1)} %get-tuple-element.19), channel_id=1, replica_groups={{0,4,8,12,16,20,24,28},{32,36,40,44,48,52,56,60},{1,5,9,13,17,21,25,29}..., dimensions={0} | all-to-all | bytes 65536 | tf_op jit(solution)/shard_map/cond/branch_0_fun/all_to_all | solution.py:285
  25.1 0.2 branch_0_fun.6
  25.3 21.5 %all_to_all.29 = bf16[16,2,512]{2,1,0:T(2,128)(2,1)S(1)} all-to-all(bf16[16,2,512]{2,1,0:T(2,128)(2,1)S(1)} %get-tuple-element.20), channel_id=1, replica_groups=mesh['inline'=8,'window'=16,'replica'=4] {'window'}, dimensions={0} | all-to-all | bytes 65536 | tf_op jit(solution)/shard_map/cond/branch_0_fun/all_to_all | solution.py:285
  46.9 3.6 %all-to-all-start.2 = ((bf16[8,128,512]{2,1,0:T(8,128)(2,1)}), bf16[8,128,512]{2,1,0:T(8,128)(2,1)S(1)}, u32[]{:S(2)}, u32[]{:S(2)}) async-start(bf16[8,128,512]{2,1,0:T(8,128)(2,1)} %get-tuple-element.21), calls=%async_computation.2 | async-start | bytes 2097152 | tf_op jit(solution)/shard_map/cond/branch_0_fun/all_to_all | solution.py:285
  50.5 4.6 %collective-permute-start = (bf16[32,512]{1,0:T(8,128)(2,1)S(1)}, bf16[32,512]{1,0:T(8,128)(2,1)S(1)}, u32[]{:S(2)}, u32[]{:S(2)}) collective-permute-start(bf16[32,512]{1,0:T(8,128)(2,1)S(1)} %reshape.10), channel_id=1, source_target_pairs={{0,64},{64,0},{128,192},{192,128},{256,320},{320,256},{384,448},{4... | collective-permute-start | bytes 98312 | tf_op jit(solution)/shard_map/cond/branch_0_fun/ppermute | solution.py:327
  55.1 1.5 %collective-permute-done = bf16[32,512]{1,0:T(8,128)(2,1)S(1)} collective-permute-done((bf16[32,512]{1,0:T(8,128)(2,1)S(1)}, bf16[32,512]{1,0:T(8,128)(2,1)S(1)}, u32[]{:S(2)}, u32[]{:S(2)}) %collective-permute-start) | collective-permute-done | bytes 32800 | tf_op jit(solution)/shard_map/cond/branch_0_fun/ppermute | solution.py:327
  56.7 3.2 %collective-permute-start.1 = (bf16[64,512]{1,0:T(8,128)(2,1)S(1)}, bf16[64,512]{1,0:T(8,128)(2,1)S(1)}, u32[]{:S(2)}, u32[]{:S(2)}) collective-permute-start(bf16[64,512]{1,0:T(8,128)(2,1)S(1)} %pad_maximum_fusion.2), channel_id=1, source_target_pairs={{0,128},{64,192},{128,0},{192,64},{256,384},{320,448},{384,256},{4... | collective-permute-start | bytes 196616 | tf_op jit(solution)/shard_map/cond/branch_0_fun/ppermute | solution.py:327
  59.9 2.1 %collective-permute-done.1 = bf16[64,512]{1,0:T(8,128)(2,1)S(1)} collective-permute-done((bf16[64,512]{1,0:T(8,128)(2,1)S(1)}, bf16[64,512]{1,0:T(8,128)(2,1)S(1)}, u32[]{:S(2)}, u32[]{:S(2)}) %collective-permute-start.1) | collective-permute-done | bytes 65568 | tf_op jit(solution)/shard_map/cond/branch_0_fun/ppermute | solution.py:327
  62.0 4.8 %collective-permute-start.2 = (bf16[128,512]{1,0:T(8,128)(2,1)S(1)}, bf16[128,512]{1,0:T(8,128)(2,1)S(1)}, u32[]{:S(2)}, u32[]{:S(2)}) collective-permute-start(bf16[128,512]{1,0:T(8,128)(2,1)S(1)} %pad_maximum_fusion.1), channel_id=1, source_target_pairs={{0,256},{64,320},{128,384},{192,448},{256,0},{320,64},{384,128},{4... | collective-permute-start | bytes 393224 | tf_op jit(solution)/shard_map/cond/branch_0_fun/ppermute | solution.py:327
  66.8 0.0 copy-start
  66.8 2.1 %branch_0_fun.8 = (bf16[512,512]{1,0:T(8,128)(2,1)S(1)}, bf16[512,512]{1,0:T(8,128)(2,1)S(1)}) custom-call(bf16[512,1536]{1,0:T(8,128)(2,1)} %get-tuple-element.24.w_ref.wq_ref.wv_ref.wk_ref, bf16[512,1536]{1,0:T(8,128)(2,1)} %get-tuple-element.24.w_ref.wq_ref.wv_ref.wk_ref), custom_call_target="tpu_custom_call" | custom-call | flops 600000000 | bytes 2097152 | tf_op jit(solution)/shard_map/cond/branch_0_fun/pallas_call | solution.py:79
  68.9 0.0 copy-start.2
  68.9 0.6 collective-permute-done.2
  69.5 0.0 copy-done
  69.5 1.4 %branch_0_fun.7.glob_ref = f32[2,8,512]{2,1,0:T(8,128)S(1)} custom-call(bf16[256,512]{1,0:T(8,128)(2,1)S(1)} %pad_maximum_fusion.all_ref, f32[2,8,512]{2,1,0:T(8,128)S(1)} %get-tuple-element.22.own_ref.car_ref, bf16[512,1536]{1,0:T(8,128)(2,1)S(1)} %copy-done), custom_call_target="tpu_custom_call" | custom-call | flops 400000000 | bytes 2097152 | tf_op jit(solution)/shard_map/cond/branch_0_fun/pallas_call | solution.py:228
  70.9 9.3 %all-to-all-done.2.x_ref = bf16[8,128,512]{2,1,0:T(8,128)(2,1)S(1)} async-done(((bf16[8,128,512]{2,1,0:T(8,128)(2,1)}), bf16[8,128,512]{2,1,0:T(8,128)(2,1)S(1)}, u32[]{:S(2)}, u32[]{:S(2)}) %all-to-all-start.2) | async-done | bytes 1048608 | tf_op jit(solution)/shard_map/cond/branch_0_fun/all_to_all | solution.py:285
  80.2 0.0 copy-done.2
  80.2 12.9 %branch_0_fun.9 = bf16[8,128,512]{2,1,0:T(8,128)(2,1)S(1)} custom-call(bf16[8,128,512]{2,1,0:T(8,128)(2,1)S(1)} %all-to-all-done.2.x_ref, f32[2,8,512]{2,1,0:T(8,128)S(1)} %get-tuple-element.22.own_ref.car_ref, f32[2,8,512]{2,1,0:T(8,128)S(1)} %branch_0_fun.7.glob_ref, bf16[512,1536]{1,0:T(8,128)(2,1)} %get-tuple-element.24.w_ref.wq_ref.wv_ref.wk_ref, ...), custom_call_target="tpu_custom_call" | custom-call | flops 16999999488 | bytes 6291456 | tf_op jit(solution)/shard_map/cond/branch_0_fun/pallas_call | solution.py:192
  93.1 40.7 %all_to_all.30 = bf16[8,128,512]{2,1,0:T(8,128)(2,1)} all-to-all(bf16[8,128,512]{2,1,0:T(8,128)(2,1)S(1)} %branch_0_fun.9), channel_id=1, replica_groups={{0,4,8,12,16,20,24,28},{32,36,40,44,48,52,56,60},{1,5,9,13,17,21,25,29}..., dimensions={0} | all-to-all | bytes 2097152 | tf_op jit(solution)/shard_map/cond/branch_0_fun/all_to_all | solution.py:285
  134.0 2.1 %shard_map.37 = bf16[8,128,512]{2,1,0:T(8,128)(2,1)} custom-call(bf16[8,128,512]{2,1,0:T(8,128)(2,1)} %get-tuple-element.39.x_ref, f32[8,2,512]{2,1,0:T(2,128)S(1)} %get-tuple-element.40.g_ref), custom_call_target="tpu_custom_call" | custom-call | flops 1000000 | bytes 2097152 | tf_op jit(solution)/shard_map/pallas_call | solution.py:273
  (5 shorter events, 0.1 us)
Async XLA Ops:
  46.9 33.4 %all-to-all-start.2 = ((bf16[8,128,512]{2,1,0:T(8,128)(2,1)}), bf16[8,128,512]{2,1,0:T(8,128)(2,1)S(1)}, u32[]{:S(2)}, u32[]{:S(2)}) async-start(bf16[8,128,512]{2,1,0:T(8,128)(2,1)} %get-tuple-element.21), calls=%async_computation.2 | async-start | bytes 2097152 | tf_op jit(solution)/shard_map/cond/branch_0_fun/all_to_all | solution.py:285
  50.5 6.2 %collective-permute-start = (bf16[32,512]{1,0:T(8,128)(2,1)S(1)}, bf16[32,512]{1,0:T(8,128)(2,1)S(1)}, u32[]{:S(2)}, u32[]{:S(2)}) collective-permute-start(bf16[32,512]{1,0:T(8,128)(2,1)S(1)} %reshape.10), channel_id=1, source_target_pairs={{0,64},{64,0},{128,192},{192,128},{256,320},{320,256},{384,448},{4... | collective-permute-start | bytes 98312 | tf_op jit(solution)/shard_map/cond/branch_0_fun/ppermute | solution.py:327
  56.7 5.3 %collective-permute-start.1 = (bf16[64,512]{1,0:T(8,128)(2,1)S(1)}, bf16[64,512]{1,0:T(8,128)(2,1)S(1)}, u32[]{:S(2)}, u32[]{:S(2)}) collective-permute-start(bf16[64,512]{1,0:T(8,128)(2,1)S(1)} %pad_maximum_fusion.2), channel_id=1, source_target_pairs={{0,128},{64,192},{128,0},{192,64},{256,384},{320,448},{384,256},{4... | collective-permute-start | bytes 196616 | tf_op jit(solution)/shard_map/cond/branch_0_fun/ppermute | solution.py:327
  62.0 7.5 %collective-permute-start.2 = (bf16[128,512]{1,0:T(8,128)(2,1)S(1)}, bf16[128,512]{1,0:T(8,128)(2,1)S(1)}, u32[]{:S(2)}, u32[]{:S(2)}) collective-permute-start(bf16[128,512]{1,0:T(8,128)(2,1)S(1)} %pad_maximum_fusion.1), channel_id=1, source_target_pairs={{0,256},{64,320},{128,384},{192,448},{256,0},{320,64},{384,128},{4... | collective-permute-start | bytes 393224 | tf_op jit(solution)/shard_map/cond/branch_0_fun/ppermute | solution.py:327
  66.8 2.7 %copy-start = (bf16[512,1536]{1,0:T(8,128)(2,1)S(1)}, bf16[512,1536]{1,0:T(8,128)(2,1)}, u32[]{:S(2)}) copy-start(bf16[512,1536]{1,0:T(8,128)(2,1)} %get-tuple-element.24.w_ref.wq_ref.wv_ref.wk_ref) | copy-start | bytes 4718596 | tf_op jit(solution)/shard_map/cond
  68.9 11.4 %copy-start.2 = (bf16[512,512]{1,0:T(8,128)(2,1)S(1)}, bf16[512,512]{1,0:T(8,128)(2,1)}, u32[]{:S(2)}) copy-start(bf16[512,512]{1,0:T(8,128)(2,1)} %get-tuple-element.27.wo_ref) | copy-start | bytes 1572868 | tf_op jit(solution)/shard_map/cond
